TPU v7x, 256 devices: a whole 4x4x8 slice. The times are simulated.
256 devices in a mesh: space: 4 (over y), energy: 64 (over x, z, core).
Axes of the slice: x: 4, y: 4, z: 8, core: 2. Of those that a mesh axis runs over, the one named last changes fastest.
Arguments:
- ham_blocks: float32 [4, 2, 256, 256], P('space'), may hold values from -0.1875 to 0.1875
- hopping: float32 [4, 2, 256, 256], P('space'), may hold values from -0.1875 to 0.1875
- energy: float32 [64], P('energy'), may hold values from -1.5 to 1.5
- broadening: float32 [64], P('energy'), may hold values from 0.05 to 0.2
- contact: float32 [64], P('energy'), may hold values from 0.5 to 2
- phonon_offset: int32 [64, 8], P('energy'), may hold values from -4 to 4, as said below
- phonon_weight: float32 [64, 8], P('energy'), may hold values from 0.1 to 0.4
Outputs:
- green: float32 [64, 4, 2, 256, 256], P('energy', 'space')
- self_energy: float32 [64, 4, 2, 256, 256], P('energy', 'space')
Inputs may be any that keep to these rules, and one draw needn't show every extreme that they name: `phonon_offset`: for every energy, entry 0 is +4 and entry 1 is -4 (absorption and emission of the optical phonon); every other entry is nonzero with magnitude below 4.
All inputs are finite; a program needn't handle non-finite values.
Results may differ from a plain program's by a relative error of at most 0.00065.
Values sent between devices are 32-bit elements; how exact they have to be, the bound alone decides.
A program may use at most 128 MiB of HBM per device.

v0:
```python
import jax
import jax.numpy as jnp
from jax import lax
from jax.sharding import PartitionSpec as P

SHIFT = 4


highest = lax.Precision.HIGHEST


def passed_along(array, axis, by):
    peers = lax.axis_size(axis)
    pairs = [(i, i + by) for i in range(peers) if 0 <= i + by < peers]
    return lax.ppermute(array, axis, pairs)


def complex_product(first_factor, second_factor):
    real_part = jnp.dot(first_factor[0], second_factor[0], precision=highest) - jnp.dot(
        first_factor[1], second_factor[1], precision=highest
    )
    imag_part = jnp.dot(first_factor[0], second_factor[1], precision=highest) + jnp.dot(
        first_factor[1], second_factor[0], precision=highest
    )
    return jnp.stack([real_part, imag_part])


def adjoint(matrix):
    return jnp.stack([matrix[0].T, -matrix[1].T])


def complex_inverse(matrix):
    block_order = matrix.shape[1]
    real_block = matrix[0]
    imag_block = matrix[1]
    gram_real = jnp.dot(real_block.T, real_block, precision=highest) + jnp.dot(
        imag_block.T, imag_block, precision=highest
    )
    gram_imag = jnp.dot(real_block.T, imag_block, precision=highest) - jnp.dot(
        imag_block.T, real_block, precision=highest
    )
    system = jnp.concatenate(
        [jnp.concatenate([gram_real, -gram_imag], 1), jnp.concatenate([gram_imag, gram_real], 1)], 0
    )
    factor = jnp.linalg.cholesky(system)
    target = jnp.concatenate([real_block.T, -imag_block.T], 0)
    solved = jax.scipy.linalg.cho_solve((factor, True), target)
    return jnp.stack([solved[:block_order], solved[block_order:]])


def per_device(ham_blocks, hopping, energy, broadening, contact, phonon_offset, phonon_weight):
    block_count = ham_blocks.shape[0]
    block_order = ham_blocks.shape[2]
    places = lax.axis_size("space")
    position = lax.axis_index("space")
    flipped = jnp.stack(
        [jnp.swapaxes(ham_blocks[:, 0], 1, 2), -jnp.swapaxes(ham_blocks[:, 1], 1, 2)], 1
    )
    hermitian = 0.5 * (ham_blocks + flipped)
    identity = jnp.eye(block_order, dtype=jnp.float32)
    naught = jnp.zeros((block_order, block_order), jnp.float32)
    vacant = jnp.stack([naught, naught])
    lead_gram = complex_product(hopping[0], adjoint(hopping[0]))
    lead_term = jnp.stack([-lead_gram[1], lead_gram[0]])
    end_term = jnp.stack([naught, identity])
    shifted = jnp.stack([energy[0] * identity, broadening[0] * identity])
    blocks = shifted[None] - hermitian
    at_start = jnp.where(position == 0, 1.0, 0.0).astype(jnp.float32)
    at_end = jnp.where(position == places - 1, 1.0, 0.0).astype(jnp.float32)
    blocks = blocks.at[0].add(at_start * (contact[0] * lead_term))
    blocks = blocks.at[block_count - 1].add(at_end * (contact[0] * end_term))
    incoming = vacant
    for sweep_round in range(places - 1):
        carry_current = complex_inverse(blocks[0] - incoming)
        finished = carry_current
        arrived = passed_along(finished, "space", 1)
        incoming = complex_product(adjoint(hopping[0]), complex_product(arrived, hopping[0]))
    sigma_terms = incoming
    incoming = vacant
    for sweep_round in range(places - 1):
        current = complex_inverse(blocks[block_count - 1] - incoming)
        finished = current
        leaving = complex_product(hopping[0], complex_product(finished, adjoint(hopping[0])))
        incoming = passed_along(leaving, "space", -1)
    greens = jnp.stack([complex_inverse(blocks[0] - sigma_terms - incoming)])
    offsets = phonon_offset[0]
    weights = phonon_weight[0]
    accumulated = jnp.zeros_like(greens)
    for offset_value in list(range(-SHIFT, 0)) + list(range(1, SHIFT + 1)):
        partner = passed_along(greens, "energy", -offset_value)
        accumulated = (
            accumulated
            + jnp.sum(jnp.where(offsets == offset_value, weights, jnp.zeros_like(weights)))
            * partner
        )
    return (greens[None], accumulated[None])


def solution(mesh):
    placed = (
        P("space", None, None, None),
        P("space", None, None, None),
        P("energy"),
        P("energy"),
        P("energy"),
        P("energy", None),
        P("energy", None),
    )
    return jax.shard_map(
        per_device,
        mesh=mesh,
        in_specs=placed,
        out_specs=(P("energy", "space", None, None, None), P("energy", "space", None, None, None)),
        check_vma=False,
    )
```

profile of v0, /device:TPU:1, one launch (start us, length us, event | category | flops | bytes accessed | tf_op | source)
XLA Modules:
  0.0 1144.2 jit_solution(3978919020009768500)
XLA Ops:
  19.0 11.7 %cholesky.638 = f32[128,128]{1,0:T(8,128)S(1)} custom-call(f32[128,128]{1,0:T(8,128)S(1)} %cholesky.1066), custom_call_target="Cholesky" | custom-call | tf_op jit(solution)/shard_map/jit(cholesky)/cholesky | solution.py:45
  45.0 11.9 %cholesky.657 = f32[128,128]{1,0:T(8,128)S(1)} custom-call(f32[128,128]{1,0:T(8,128)S(1)} %cholesky.1070), custom_call_target="Cholesky" | custom-call | tf_op jit(solution)/shard_map/jit(cholesky)/cholesky | solution.py:45
  70.9 11.7 %cholesky.678 = f32[128,128]{1,0:T(8,128)S(1)} custom-call(f32[128,128]{1,0:T(8,128)S(1)} %cholesky.1075), custom_call_target="Cholesky" | custom-call | tf_op jit(solution)/shard_map/jit(cholesky)/cholesky | solution.py:45
  96.0 11.9 %cholesky.695 = f32[128,128]{1,0:T(8,128)S(1)} custom-call(f32[128,128]{1,0:T(8,128)S(1)} %convolution_subtract_fusion.69), custom_call_target="Cholesky" | custom-call | tf_op jit(solution)/shard_map/jit(cholesky)/cholesky | solution.py:45
  126.1 40.1 %custom-call.48 = f32[4,128,128]{1,2,0:T(8,128)S(1)} custom-call(f32[4,128,128]{2,1,0:T(8,128)} %copy-done.48), custom_call_target="InvertDiagBlocksLowerTriangular" | custom-call | tf_op jit(solution)/shard_map/jit(_cho_solve)/triangular_solve | solution.py:47
  208.1 11.9 %cholesky.710 = f32[128,128]{1,0:T(8,128)S(1)} custom-call(f32[128,128]{1,0:T(8,128)S(1)} %cholesky.1079), custom_call_target="Cholesky" | custom-call | tf_op jit(solution)/shard_map/jit(cholesky)/cholesky | solution.py:45
  234.2 11.7 %cholesky.729 = f32[128,128]{1,0:T(8,128)S(1)} custom-call(f32[128,128]{1,0:T(8,128)S(1)} %cholesky.1083), custom_call_target="Cholesky" | custom-call | tf_op jit(solution)/shard_map/jit(cholesky)/cholesky | solution.py:45
  260.0 12.1 %cholesky.750 = f32[128,128]{1,0:T(8,128)S(1)} custom-call(f32[128,128]{1,0:T(8,128)S(1)} %cholesky.1088), custom_call_target="Cholesky" | custom-call | tf_op jit(solution)/shard_map/jit(cholesky)/cholesky | solution.py:45
  285.6 11.7 %cholesky.767 = f32[128,128]{1,0:T(8,128)S(1)} custom-call(f32[128,128]{1,0:T(8,128)S(1)} %convolution_subtract_fusion.68), custom_call_target="Cholesky" | custom-call | tf_op jit(solution)/shard_map/jit(cholesky)/cholesky | solution.py:45
  315.6 40.1 %custom-call.52 = f32[4,128,128]{1,2,0:T(8,128)S(1)} custom-call(f32[4,128,128]{2,1,0:T(8,128)} %copy-done.49), custom_call_target="InvertDiagBlocksLowerTriangular" | custom-call | tf_op jit(solution)/shard_map/jit(_cho_solve)/triangular_solve | solution.py:47
  401.6 11.7 %cholesky.854 = f32[128,128]{1,0:T(8,128)S(1)} custom-call(f32[128,128]{1,0:T(8,128)S(1)} %cholesky.1105), custom_call_target="Cholesky" | custom-call | tf_op jit(solution)/shard_map/jit(cholesky)/cholesky | solution.py:45
  428.4 11.7 %cholesky.873 = f32[128,128]{1,0:T(8,128)S(1)} custom-call(f32[128,128]{1,0:T(8,128)S(1)} %cholesky.1109), custom_call_target="Cholesky" | custom-call | tf_op jit(solution)/shard_map/jit(cholesky)/cholesky | solution.py:45
  454.3 12.1 %cholesky.894 = f32[128,128]{1,0:T(8,128)S(1)} custom-call(f32[128,128]{1,0:T(8,128)S(1)} %cholesky.1114), custom_call_target="Cholesky" | custom-call | tf_op jit(solution)/shard_map/jit(cholesky)/cholesky | solution.py:45
  479.8 11.7 %cholesky.911 = f32[128,128]{1,0:T(8,128)S(1)} custom-call(f32[128,128]{1,0:T(8,128)S(1)} %convolution_subtract_fusion.66), custom_call_target="Cholesky" | custom-call | tf_op jit(solution)/shard_map/jit(cholesky)/cholesky | solution.py:45
  509.8 40.3 %custom-call.60 = f32[4,128,128]{1,2,0:T(8,128)S(1)} custom-call(f32[4,128,128]{2,1,0:T(8,128)} %copy-done.50), custom_call_target="InvertDiagBlocksLowerTriangular" | custom-call | tf_op jit(solution)/shard_map/jit(_cho_solve)/triangular_solve | solution.py:47
  569.6 11.7 %cholesky.782 = f32[128,128]{1,0:T(8,128)S(1)} custom-call(f32[128,128]{1,0:T(8,128)S(1)} %cholesky.1092), custom_call_target="Cholesky" | custom-call | tf_op jit(solution)/shard_map/jit(cholesky)/cholesky | solution.py:45
  596.0 11.7 %cholesky.801 = f32[128,128]{1,0:T(8,128)S(1)} custom-call(f32[128,128]{1,0:T(8,128)S(1)} %cholesky.1096), custom_call_target="Cholesky" | custom-call | tf_op jit(solution)/shard_map/jit(cholesky)/cholesky | solution.py:45
  621.9 11.7 %cholesky.822 = f32[128,128]{1,0:T(8,128)S(1)} custom-call(f32[128,128]{1,0:T(8,128)S(1)} %cholesky.1101), custom_call_target="Cholesky" | custom-call | tf_op jit(solution)/shard_map/jit(cholesky)/cholesky | solution.py:45
  647.1 11.7 %cholesky.839 = f32[128,128]{1,0:T(8,128)S(1)} custom-call(f32[128,128]{1,0:T(8,128)S(1)} %convolution_subtract_fusion.67), custom_call_target="Cholesky" | custom-call | tf_op jit(solution)/shard_map/jit(cholesky)/cholesky | solution.py:45
  665.0 11.7 %while.16 = (s32[]{:T(128)}, f32[512,512]{1,0:T(8,128)}, s32[4,2]{0,1:T(2,128)S(1)}, f32[4,128,128]{2,1,0:T(8,128)S(1)}, s32[]{:T(128)}) while((s32[]{:T(128)}, f32[512,512]{1,0:T(8,128)}, s32[4,2]{0,1:T(2,128)S(1)}, f32[4,128,128]{2,1,0:T(8,128)S(1)}, s32[]{:T(128)}) %tuple.183), condition=%wide.while_cond.2.clone.1, body=%wide.while_body.2.clone.1.sunk | while | flops 2 | bytes 131181 | solution.py:47
  677.4 40.1 %custom-call.56 = f32[4,128,128]{1,2,0:T(8,128)S(1)} custom-call(f32[4,128,128]{2,1,0:T(8,128)} %copy-done.51), custom_call_target="InvertDiagBlocksLowerTriangular" | custom-call | tf_op jit(solution)/shard_map/jit(_cho_solve)/triangular_solve | solution.py:47
  751.6 11.7 %cholesky.926 = f32[128,128]{1,0:T(8,128)S(1)} custom-call(f32[128,128]{1,0:T(8,128)S(1)} %cholesky.1118), custom_call_target="Cholesky" | custom-call | tf_op jit(solution)/shard_map/jit(cholesky)/cholesky | solution.py:45
  777.5 11.9 %cholesky.945 = f32[128,128]{1,0:T(8,128)S(1)} custom-call(f32[128,128]{1,0:T(8,128)S(1)} %cholesky.1122), custom_call_target="Cholesky" | custom-call | tf_op jit(solution)/shard_map/jit(cholesky)/cholesky | solution.py:45
  803.6 11.7 %cholesky.966 = f32[128,128]{1,0:T(8,128)S(1)} custom-call(f32[128,128]{1,0:T(8,128)S(1)} %cholesky.1127), custom_call_target="Cholesky" | custom-call | tf_op jit(solution)/shard_map/jit(cholesky)/cholesky | solution.py:45
  828.7 12.1 %cholesky.983 = f32[128,128]{1,0:T(8,128)S(1)} custom-call(f32[128,128]{1,0:T(8,128)S(1)} %convolution_subtract_fusion.65), custom_call_target="Cholesky" | custom-call | tf_op jit(solution)/shard_map/jit(cholesky)/cholesky | solution.py:45
  859.3 40.1 %custom-call.64 = f32[4,128,128]{1,2,0:T(8,128)S(1)} custom-call(f32[4,128,128]{2,1,0:T(8,128)} %copy-done.52), custom_call_target="InvertDiagBlocksLowerTriangular" | custom-call | tf_op jit(solution)/shard_map/jit(_cho_solve)/triangular_solve | solution.py:47
  927.1 11.7 %cholesky.998 = f32[128,128]{1,0:T(8,128)S(1)} custom-call(f32[128,128]{1,0:T(8,128)S(1)} %cholesky.1131), custom_call_target="Cholesky" | custom-call | tf_op jit(solution)/shard_map/jit(cholesky)/cholesky | solution.py:45
  949.5 11.9 %cholesky.1017 = f32[128,128]{1,0:T(8,128)S(1)} custom-call(f32[128,128]{1,0:T(8,128)S(1)} %cholesky.1135), custom_call_target="Cholesky" | custom-call | tf_op jit(solution)/shard_map/jit(cholesky)/cholesky | solution.py:45
  973.2 11.7 %cholesky.1038 = f32[128,128]{1,0:T(8,128)S(1)} custom-call(f32[128,128]{1,0:T(8,128)S(1)} %cholesky.1140), custom_call_target="Cholesky" | custom-call | tf_op jit(solution)/shard_map/jit(cholesky)/cholesky | solution.py:45
  996.3 11.7 %cholesky.1055 = f32[128,128]{1,0:T(8,128)S(1)} custom-call(f32[128,128]{1,0:T(8,128)S(1)} %convolution_subtract_fusion.64), custom_call_target="Cholesky" | custom-call | tf_op jit(solution)/shard_map/jit(cholesky)/cholesky | solution.py:45
  1019.4 39.3 %custom-call.68 = f32[4,128,128]{1,2,0:T(8,128)S(1)} custom-call(f32[4,128,128]{2,1,0:T(8,128)S(1)} %get-tuple-element.71), custom_call_target="InvertDiagBlocksLowerTriangular" | custom-call | tf_op jit(solution)/shard_map/jit(_cho_solve)/triangular_solve | solution.py:47
  1091.0 32.2 %collective-permute-done.12 = f32[1,2,256,256]{3,2,1,0:T(8,128)S(1)} collective-permute-done((f32[1,2,256,256]{3,2,1,0:T(8,128)S(1)}, f32[1,2,256,256]{3,2,1,0:T(8,128)S(1)}, u32[]{:S(2)}, u32[]{:S(2)}) %collective-permute-start.12) | collective-permute-done | bytes 524320 | tf_op jit(solution)/shard_map/ppermute | solution.py:15
  (570 shorter events, 621.2 us)
Async XLA Ops:
  14.0 2.6 copy-start.14
  14.0 2.6 copy-start.22
  114.2 52.1 %copy-start.35 = (f32[256,256]{1,0:T(8,128)S(1)}, f32[256,256]{1,0:T(8,128)}, u32[]{:S(2)}) copy-start(f32[256,256]{1,0:T(8,128)} %slice_bitcast_fusion.48) | copy-start | bytes 786436
  166.3 6.0 copy-start.28
  175.0 14.9 %collective-permute-start = (f32[2,256,256]{2,1,0:T(8,128)}, f32[2,256,256]{2,1,0:T(8,128)}, u32[]{:S(2)}, u32[]{:S(2)}) collective-permute-start(f32[2,256,256]{2,1,0:T(8,128)} %pad_maximum_fusion), channel_id=1, source_target_pairs={{0,64},{64,128},{128,192},{1,65},{65,129},{129,193},{2,66},{66,130... | collective-permute-start | bytes 1572872 | tf_op jit(solution)/shard_map/ppermute | solution.py:15
  355.7 2.9 copy-start.2
  363.8 5.7 copy-start.38
  364.6 14.1 %collective-permute-start.1 = (f32[2,256,256]{2,1,0:T(8,128)}, f32[2,256,256]{2,1,0:T(8,128)}, u32[]{:S(2)}, u32[]{:S(2)}) collective-permute-start(f32[2,256,256]{2,1,0:T(8,128)} %pad_maximum_fusion.1), channel_id=1, source_target_pairs={{0,64},{64,128},{128,192},{1,65},{65,129},{129,193},{2,66},{66,130... | collective-permute-start | bytes 1572872 | tf_op jit(solution)/shard_map/ppermute | solution.py:15
  371.3 15.1 %collective-permute-start.3 = (f32[2,256,256]{1,2,0:T(8,128)S(1)}, f32[2,256,256]{1,2,0:T(8,128)}, u32[]{:S(2)}, u32[]{:S(2)}) collective-permute-start(f32[2,256,256]{1,2,0:T(8,128)S(1)} %pad_maximum_fusion.3), channel_id=1, source_target_pairs={{64,0},{128,64},{192,128},{65,1},{129,65},{193,129},{66,2},{130,66... | collective-permute-start | bytes 1572872 | tf_op jit(solution)/shard_map/ppermute | solution.py:15
  428.4 23.5 %copy-start.47 = (f32[384,128]{1,0:T(8,128)S(1)}, f32[384,128]{1,0:T(8,128)}, u32[]{:S(2)}) copy-start(f32[384,128]{1,0:T(8,128)} %copy-done.46) | copy-start | bytes 589828
  550.1 2.5 copy-start.29
  550.1 3.7 copy-start.3
  564.5 2.6 copy-start.18
  564.5 2.6 copy-start.20
  665.0 52.6 %copy-start.34 = (f32[256,256]{1,0:T(8,128)S(1)}, f32[256,256]{1,0:T(8,128)}, u32[]{:S(2)}) copy-start(f32[256,256]{1,0:T(8,128)} %slice_bitcast_fusion.46) | copy-start | bytes 786436
  728.3 13.9 %collective-permute-start.4 = (f32[2,256,256]{1,2,0:T(8,128)S(1)}, f32[2,256,256]{1,2,0:T(8,128)S(1)}, u32[]{:S(2)}, u32[]{:S(2)}) collective-permute-start(f32[2,256,256]{1,2,0:T(8,128)S(1)} %pad_maximum_fusion.4), channel_id=1, source_target_pairs={{64,0},{128,64},{192,128},{65,1},{129,65},{193,129},{66,2},{130,66... | collective-permute-start | bytes 1572872 | tf_op jit(solution)/shard_map/ppermute | solution.py:15
  730.8 174.9 %collective-permute-start.2 = (f32[2,256,256]{2,1,0:T(8,128)}, f32[2,256,256]{2,1,0:T(8,128)}, u32[]{:S(2)}, u32[]{:S(2)}) collective-permute-start(f32[2,256,256]{2,1,0:T(8,128)} %pad_maximum_fusion.2), channel_id=1, source_target_pairs={{0,64},{64,128},{128,192},{1,65},{65,129},{129,193},{2,66},{66,130... | collective-permute-start | bytes 1572872 | tf_op jit(solution)/shard_map/ppermute | solution.py:15
  844.6 56.6 %copy-start.44 = (f32[256,256]{1,0:T(8,128)S(1)}, f32[256,256]{1,0:T(8,128)}, u32[]{:S(2)}) copy-start(f32[256,256]{1,0:T(8,128)} %negate_bitcast_fusion.1) | copy-start | bytes 786436
  847.0 52.4 %copy-start.36 = (f32[256,256]{1,0:T(8,128)S(1)}, f32[256,256]{1,0:T(8,128)}, u32[]{:S(2)}) copy-start(f32[256,256]{1,0:T(8,128)} %slice_bitcast_fusion.44) | copy-start | bytes 786436
  912.3 12.2 %collective-permute-start.5 = (f32[2,256,256]{1,2,0:T(8,128)S(1)}, f32[2,256,256]{1,2,0:T(8,128)S(1)}, u32[]{:S(2)}, u32[]{:S(2)}) collective-permute-start(f32[2,256,256]{1,2,0:T(8,128)S(1)} %pad_maximum_fusion.5), channel_id=1, source_target_pairs={{64,0},{128,64},{192,128},{65,1},{129,65},{193,129},{66,2},{130,66... | collective-permute-start | bytes 1572872 | tf_op jit(solution)/shard_map/ppermute | solution.py:15
  927.1 11.7 %copy-start.11 = (f32[512,512]{1,0:T(8,128)}, f32[512,512]{1,0:T(8,128)S(1)}, u32[]{:S(2)}) copy-start(f32[512,512]{1,0:T(8,128)S(1)} %fusion.15) | copy-start | bytes 3145732
  938.9 9.9 copy-start.12
  1064.2 60.9 %copy-start.53 = (f32[1,8]{1,0:T(1,128)S(1)}, f32[1,8]{1,0:T(1,128)}, u32[]{:S(2)}) copy-start(f32[1,8]{1,0:T(1,128)} %param.20) | copy-start | bytes 100
  1064.2 60.9 %copy-start.54 = (s32[1,8]{1,0:T(1,128)S(1)}, s32[1,8]{1,0:T(1,128)}, u32[]{:S(2)}) copy-start(s32[1,8]{1,0:T(1,128)} %param.19) | copy-start | bytes 100
  1064.2 18.3 %collective-permute-start.10 = (f32[1,2,256,256]{3,2,1,0:T(8,128)S(1)}, f32[1,2,256,256]{3,2,1,0:T(8,128)S(1)}, u32[]{:S(2)}, u32[]{:S(2)}) collective-permute-start(f32[1,2,256,256]{3,2,1,0:T(8,128)S(1)} %get-tuple-element.140), channel_id=1, source_target_pairs={{1,0},{2,1},{3,2},{4,3},{5,4},{6,5},{7,6},{8,7},{9,8},{10,9},{11,1... | collective-permute-start | bytes 1572872 | tf_op jit(solution)/shard_map/ppermute | solution.py:15
  1070.3 17.1 %collective-permute-start.11 = (f32[1,2,256,256]{3,2,1,0:T(8,128)S(1)}, f32[1,2,256,256]{3,2,1,0:T(8,128)S(1)}, u32[]{:S(2)}, u32[]{:S(2)}) collective-permute-start(f32[1,2,256,256]{3,2,1,0:T(8,128)S(1)} %get-tuple-element.140), channel_id=1, source_target_pairs={{2,0},{3,1},{4,2},{5,3},{6,4},{7,5},{8,6},{9,7},{10,8},{11,9},{12,... | collective-permute-start | bytes 1572872 | tf_op jit(solution)/shard_map/ppermute | solution.py:15
  1071.6 51.6 %collective-permute-start.12 = (f32[1,2,256,256]{3,2,1,0:T(8,128)S(1)}, f32[1,2,256,256]{3,2,1,0:T(8,128)S(1)}, u32[]{:S(2)}, u32[]{:S(2)}) collective-permute-start(f32[1,2,256,256]{3,2,1,0:T(8,128)S(1)} %get-tuple-element.140), channel_id=1, source_target_pairs={{3,0},{4,1},{5,2},{6,3},{7,4},{8,5},{9,6},{10,7},{11,8},{12,9},{13... | collective-permute-start | bytes 1572872 | tf_op jit(solution)/shard_map/ppermute | solution.py:15
  1072.9 54.2 %collective-permute-start.13 = (f32[1,2,256,256]{3,2,1,0:T(8,128)S(1)}, f32[1,2,256,256]{3,2,1,0:T(8,128)S(1)}, u32[]{:S(2)}, u32[]{:S(2)}) collective-permute-start(f32[1,2,256,256]{3,2,1,0:T(8,128)S(1)} %get-tuple-element.140), channel_id=1, source_target_pairs={{4,0},{5,1},{6,2},{7,3},{8,4},{9,5},{10,6},{11,7},{12,8},{13,9},{1... | collective-permute-start | bytes 1572872 | tf_op jit(solution)/shard_map/ppermute | solution.py:15
  1074.2 52.9 %collective-permute-start.6 = (f32[1,2,256,256]{3,2,1,0:T(8,128)S(1)}, f32[1,2,256,256]{3,2,1,0:T(8,128)S(1)}, u32[]{:S(2)}, u32[]{:S(2)}) collective-permute-start(f32[1,2,256,256]{3,2,1,0:T(8,128)S(1)} %get-tuple-element.140), channel_id=1, source_target_pairs={{0,4},{1,5},{2,6},{3,7},{4,8},{5,9},{6,10},{7,11},{8,12},{9,13},{1... | collective-permute-start | bytes 1572872 | tf_op jit(solution)/shard_map/ppermute | solution.py:15
  1082.5 44.6 %collective-permute-start.7 = (f32[1,2,256,256]{3,2,1,0:T(8,128)S(1)}, f32[1,2,256,256]{3,2,1,0:T(8,128)S(1)}, u32[]{:S(2)}, u32[]{:S(2)}) collective-permute-start(f32[1,2,256,256]{3,2,1,0:T(8,128)S(1)} %get-tuple-element.140), channel_id=1, source_target_pairs={{0,3},{1,4},{2,5},{3,6},{4,7},{5,8},{6,9},{7,10},{8,11},{9,12},{10... | collective-permute-start | bytes 1572872 | tf_op jit(solution)/shard_map/ppermute | solution.py:15
  1087.4 44.2 %collective-permute-start.8 = (f32[1,2,256,256]{3,2,1,0:T(8,128)S(1)}, f32[1,2,256,256]{3,2,1,0:T(8,128)S(1)}, u32[]{:S(2)}, u32[]{:S(2)}) collective-permute-start(f32[1,2,256,256]{3,2,1,0:T(8,128)S(1)} %get-tuple-element.140), channel_id=1, source_target_pairs={{0,2},{1,3},{2,4},{3,5},{4,6},{5,7},{6,8},{7,9},{8,10},{9,11},{10,... | collective-permute-start | bytes 1572872 | tf_op jit(solution)/shard_map/ppermute | solution.py:15
  1123.1 14.6 %collective-permute-start.9 = (f32[1,2,256,256]{3,2,1,0:T(8,128)S(1)}, f32[1,2,256,256]{3,2,1,0:T(8,128)S(1)}, u32[]{:S(2)}, u32[]{:S(2)}) collective-permute-start(f32[1,2,256,256]{3,2,1,0:T(8,128)S(1)} %get-tuple-element.140), channel_id=1, source_target_pairs={{0,1},{1,2},{2,3},{3,4},{4,5},{5,6},{6,7},{7,8},{8,9},{9,10},{10,1... | collective-permute-start | bytes 1572872 | tf_op jit(solution)/shard_map/ppermute | solution.py:15
  (37 other events, 35.6 us)
where the time goes:
time: 1170 us; the launch traced here: 1140 us
  other arithmetic  769 us (66%)
  matrix products  132 us (11%)
  local copies, waits for them, and re-layouts  105 us (9%)
  waiting for transfers between devices  69.1 us (6%)
  starting transfers between devices  47.4 us (4%)
  between operations  20.7 us (2%)
    another operation x90, other arithmetic, complex_inverse(): factor = jnp.linalg.cholesky(system)  486 us
    another operation x13, other arithmetic, complex_inverse(): solved = jax.scipy.linalg.cho_solve((factor, True), target)  252 us
    ppermute x14, waiting for transfers between devices, passed_along(): return lax.ppermute(array, axis, pairs)  69.1 us
    another operation x79, local copies, waits for them, and re-layouts, complex_inverse(): solved = jax.scipy.linalg.cho_solve((factor, True), target)  64.8 us
    ppermute x14, starting transfers between devices, passed_along(): return lax.ppermute(array, axis, pairs)  47.4 us
    another operation x36, matrix products, complex_inverse(): factor = jnp.linalg.cholesky(system)  41.5 us
    another operation x84, matrix products, complex_inverse(): solved = jax.scipy.linalg.cho_solve((factor, True), target)  38.3 us
  transfers between devices with their start and end apart: 14, of which 9 were waited for; matrix products, arithmetic and copies ran while one was open for 16% of the time, Pallas kernels for 0%

commit v1 on v0

v1 whole, which is shorter than its diff:
```python
import functools

import jax
import jax.numpy as jnp
from jax import lax
from jax.experimental import pallas as pl
from jax.experimental.pallas import tpu as pltpu
from jax.sharding import PartitionSpec as P

SHIFT = 4
N = 256
SUB = 32
f32 = jnp.float32
bf16 = jnp.bfloat16
VREG = (8, 128)
SLOTS = 256


def passed_along(array, axis, by):
    peers = lax.axis_size(axis)
    pairs = [(i, i + by) for i in range(peers) if 0 <= i + by < peers]
    return lax.ppermute(array, axis, pairs)


def cmul(a, b):
    return (a[0] * b[0] - a[1] * b[1], a[0] * b[1] + a[1] * b[0])


def csub(a, b):
    return (a[0] - b[0], a[1] - b[1])


def cadd(a, b):
    return (a[0] + b[0], a[1] + b[1])


def lane_of(x, l):
    return tuple(jnp.broadcast_to(a[:, l : l + 1], VREG) for a in x)


def inv2(p00, p01, p10, p11):
    det = csub(cmul(p00, p11), cmul(p01, p10))
    d = 1.0 / (det[0] * det[0] + det[1] * det[1])
    q = (det[0] * d, -det[1] * d)
    return cmul(p11, q), cmul(p01, q), cmul(p10, q), cmul(p00, q)


class Rows:
    def __init__(self, ref):
        self.ref, self.next, self.kept = ref, 0, {}

    def __call__(self, x, j):
        out = []
        for a in x:
            if id(a) not in self.kept:
                slot = self.next
                self.next = (slot + 1) % SLOTS
                self.ref[slot * 8 : slot * 8 + 8, :] = a
                self.kept[id(a)] = (slot, a)
            slot = self.kept[id(a)][0]
            out.append(self.ref[pl.ds(slot * 8 + j, 8, stride=0), :])
        return tuple(out)


def eliminate_rows(W, t, o, rows_of):
    nv = len(W[0])
    ln = lax.broadcasted_iota(jnp.int32, VREG, 1)
    sb = lax.broadcasted_iota(jnp.int32, VREG, 0)
    el = lambda c, j: rows_of(c[j // 8], j % 8)
    c0 = {0: lane_of(W[t][0], o)}
    c1 = {0: lane_of(W[t][0], o + 1)}
    D = inv2(el(c0, 0), el(c1, 0), el(c0, 1), el(c1, 1))
    for j in range(0, 8 * nv, 2):
        l = o + j
        c0 = [lane_of(W[t][v], l) for v in range(nv)]
        c1 = [lane_of(W[t][v], l + 1) for v in range(nv)]
        i00, n01, n10, i11 = D
        ar = ln == l
        ab = ar | (ln == l + 1)
        new = []
        for s in range(2):
            r0 = rows_of(W[s][j // 8], j % 8)
            r1 = rows_of(W[s][(j + 1) // 8], (j + 1) % 8)
            if s == t:
                r0 = (jnp.where(ab, jnp.where(ar, 1.0, 0.0), r0[0]), jnp.where(ab, 0.0, r0[1]))
                r1 = (jnp.where(ab, jnp.where(ar, 0.0, 1.0), r1[0]), jnp.where(ab, 0.0, r1[1]))
            s0 = csub(cmul(i00, r0), cmul(n01, r1))
            s1 = csub(cmul(i11, r1), cmul(n10, r0))
            col = []
            for v in range(nv):
                X = W[s][v]
                if s == t:
                    X = (jnp.where(ab, 0.0, X[0]), jnp.where(ab, 0.0, X[1]))
                X = csub(X, cadd(cmul(c0[v], s0), cmul(c1[v], s1)))
                if j // 8 == v:
                    X = tuple(
                        jnp.where(sb == j % 8, s0[k], jnp.where(sb == j % 8 + 1, s1[k], X[k])) for k in range(2)
                    )
                col.append(X)
            new.append(col)
        if j + 2 < 8 * nv:
            vs = sorted({j // 8, (j + 2) // 8})
            pivot = []
            for ahead in (l + 2, l + 3):
                d = {v: lane_of(W[t][v], ahead) for v in vs}
                a, c = el(d, j), el(d, j + 1)
                s0 = csub(cmul(i00, a), cmul(n01, c))
                s1 = csub(cmul(i11, c), cmul(n10, a))
                for k in (j + 2, j + 3):
                    pivot.append(csub(el(d, k), cadd(cmul(el(c0, k), s0), cmul(el(c1, k), s1))))
            D = inv2(pivot[0], pivot[2], pivot[1], pivot[3])
        W = new
    return W


def halves(x):
    high = x.astype(bf16)
    return high, (x - high.astype(f32)).astype(bf16)


def dot(a, b):
    return jnp.dot(a, b, preferred_element_type=f32)


def stacked(parts, axis):
    return jnp.concatenate(parts, axis)


def left_panel(M, o):
    ln = lax.broadcasted_iota(jnp.int32, M[0].shape, 1)
    here = (ln >= o) & (ln < o + SUB)
    both = jnp.where(here, M[0], 0.0) + pltpu.roll(jnp.where(here, M[1], 0.0), SUB, 1)
    high = both.astype(bf16).astype(f32)
    low = both - high
    return stacked([(high + pltpu.roll(low, 2 * SUB, 1)).astype(bf16), high.astype(bf16)], 1)


def right_panel(W, o):
    re = stacked([stacked([W[s][v][0] for v in range(4)], 0) for s in range(2)], 1)
    im = stacked([stacked([W[s][v][1] for v in range(4)], 0) for s in range(2)], 1)
    (rh, rl), (ih, il) = halves(re), halves(im)
    top_h, bottom_h = stacked([rh, ih], 1), stacked([-ih, rh], 1)
    top_l, bottom_l = stacked([rl, il], 1), stacked([-il, rl], 1)
    none = jnp.zeros((SUB, 2 * N), bf16)
    first = [top_h, bottom_h, top_h, bottom_h]
    second = [top_l, bottom_l, none, none]
    turn = o // SUB
    around = lambda x: [x[(g - turn) % 4] for g in range(4)]
    return stacked(around(first) + around(second), 0)


def invert(mats, rows_of):
    def tile_steps(tile, carry):
        columns = [pl.ds(pl.multiple_of(128 * tile, 128), 128), pl.ds(pl.multiple_of(128 - 128 * tile, 128), 128)]
        rows_of.kept.clear()

        def rows(q, height):
            return pl.ds(pl.multiple_of(128 * tile + SUB * q, SUB), height)

        panels = []
        for M in mats:
            whole = [[M[k][rows(0, SUB), c] for k in range(2)] for c in columns]
            panels.append([[tuple(x[8 * v : 8 * v + 8] for x in w) for v in range(4)] for w in whole])
        ln = lax.broadcasted_iota(jnp.int32, (N, 128), 1)
        for q in range(4):
            o = q * SUB
            here = (ln >= o) & (ln < o + SUB)
            lefts = [left_panel([M[k][:, columns[0]] for k in range(2)], o) for M in mats]
            strips = [left_panel([M[k][rows((q + 1) % 4, SUB), columns[0]] for k in range(2)], o) for M in mats]
            panels = [eliminate_rows(W, 0, o, rows_of) for W in panels]
            following = []
            for M, L, W in zip(mats, lefts, panels):
                R = right_panel(W, o)
                if q < 3:
                    U = dot(strips.pop(0), R)
                    nxt = []
                    for s, c in enumerate(columns):
                        pairs = []
                        for k in range(2):
                            X = M[k][rows(q + 1, SUB), c]
                            if s == 0:
                                X = jnp.where(here[:SUB], 0.0, X)
                            pairs.append(X - U[:, k * N + s * 128 : k * N + s * 128 + 128])
                        nxt.append([tuple(x[8 * v : 8 * v + 8] for x in pairs) for v in range(4)])
                    following.append(nxt)
                U = dot(L, R)
                for s, c in enumerate(columns):
                    for k in range(2):
                        X = M[k][:, c]
                        if s == 0:
                            X = jnp.where(here, 0.0, X)
                        M[k][:, c] = X - U[:, k * N + s * 128 : k * N + s * 128 + 128]
                        M[k][rows(q, SUB), c] = stacked([W[s][v][k] for v in range(4)], 0)
            panels = following
        return carry

    lax.fori_loop(0, 2, tile_steps, 0)


def product(A, B):
    ah, al = halves(stacked([A[0], A[1]], 1))
    (rh, rl), (ih, il) = halves(B[0]), halves(B[1])
    bh = stacked([stacked([rh, ih], 1), stacked([-ih, rh], 1)], 0)
    bl = stacked([stacked([rl, il], 1), stacked([-il, rl], 1)], 0)
    C = dot(ah, bh) + (dot(ah, bl) + dot(al, bh))
    return C[:, :N], C[:, N:]


def planes(ref):
    return ref.at[0], ref.at[1]


def pair(ref):
    re, im = planes(ref)
    return re[...], im[...]


def put(ref, x):
    re, im = ref if isinstance(ref, tuple) else planes(ref)
    re[...], im[...] = x


def green_kernel(place_ref, level_ref, herm_ref, gram_ref, hop_ref, out_ref, outer, work, near, side_term, scr):
    rows_of = Rows(scr)
    place = place_ref[0]
    side = place // 2
    e, eta, c = level_ref[0], level_ref[1], level_ref[2]
    eye = (lax.broadcasted_iota(jnp.int32, (N, N), 0) == lax.broadcasted_iota(jnp.int32, (N, N), 1)).astype(f32)
    near_l, near_r = jnp.where(side == 0, 5, 3), jnp.where(side == 0, 1, 7)
    far_l, far_r = jnp.where(side == 0, 3, 5), jnp.where(side == 0, 7, 1)
    mid_l, mid_r = jnp.where(side == 0, 2, 6), jnp.where(side == 0, 6, 2)

    put(planes(outer.at[0]), (e * eye - herm_ref[0, 0] - c * gram_ref[1], eta * eye - herm_ref[0, 1] + c * gram_ref[0]))
    put(planes(outer.at[1]), (e * eye - herm_ref[3, 0], (eta + c) * eye - herm_ref[3, 1]))
    invert([planes(outer.at[0]), planes(outer.at[1])], rows_of)

    def inner(i, sigma):
        return (e * eye - herm_ref[i, 0] - sigma[0], eta * eye - herm_ref[i, 1] - sigma[1])

    right = product(pair(outer.at[side]), pair(hop_ref.at[near_r]))
    put(side_term, right)
    put(near, inner(1 + side, product(pair(hop_ref.at[near_l]), right)))
    right = product(pair(outer.at[1 - side]), pair(hop_ref.at[far_r]))
    put(work, inner(2 - side, product(pair(hop_ref.at[far_l]), right)))

    def solve(step, carry):
        invert([planes(work)], rows_of)

        @pl.when(step == 0)
        def _():
            right = product(pair(work), pair(hop_ref.at[mid_r]))
            put(work, csub(pair(near), product(pair(hop_ref.at[mid_l]), right)))

        return carry

    lax.fori_loop(0, 2, solve, 0)

    @pl.when((place == 1) | (place == 2))
    def _():
        put(out_ref, pair(work))

    @pl.when((place == 0) | (place == 3))
    def _():
        own = pair(outer.at[side])
        left = product(pair(hop_ref.at[near_l]), own)
        put(out_ref, cadd(own, product(pair(side_term), product(pair(work), left))))


def green_blocks(place, levels, herm, gram, hops):
    vmem = pl.BlockSpec(memory_space=pltpu.VMEM)
    smem = pl.BlockSpec(memory_space=pltpu.SMEM)
    block = pltpu.VMEM((2, N, N), f32)
    return pl.pallas_call(
        green_kernel,
        out_shape=jax.ShapeDtypeStruct((2, N, N), f32),
        in_specs=[smem, smem, vmem, vmem, vmem],
        out_specs=vmem,
        scratch_shapes=[pltpu.VMEM((2, 2, N, N), f32), block, block, block, pltpu.VMEM((8 * SLOTS, 128), f32)],
        compiler_params=pltpu.CompilerParams(vmem_limit_bytes=48 << 20),
        cost_estimate=pl.CostEstimate(flops=10**10, bytes_accessed=10**7, transcendentals=0),
    )(place, levels, herm, gram, hops)


def adjoint(x):
    return jnp.stack([jnp.swapaxes(x[..., 0, :, :], -1, -2), -jnp.swapaxes(x[..., 1, :, :], -1, -2)], -3)


def xproduct(a, b):
    d = functools.partial(jnp.dot, precision=lax.Precision.HIGHEST)
    return jnp.stack([d(a[0], b[0]) - d(a[1], b[1]), d(a[0], b[1]) + d(a[1], b[0])])


def per_device(ham_blocks, hopping, energy, broadening, contact, phonon_offset, phonon_weight):
    place = lax.axis_index("space").astype(jnp.int32).reshape(1)
    ham = lax.all_gather(ham_blocks[0], "space")
    hop = lax.all_gather(hopping[0], "space")
    herm = 0.5 * (ham + adjoint(ham))
    hops = jnp.concatenate([hop, adjoint(hop)], 0)
    gram = xproduct(hops[0], hops[4])
    levels = jnp.concatenate([energy, broadening, contact])
    green = green_blocks(place, levels, herm, gram, hops)
    offsets = phonon_offset[0]
    weights = phonon_weight[0]
    total = jnp.zeros_like(green)
    for offset in list(range(-SHIFT, 0)) + list(range(1, SHIFT + 1)):
        partner = passed_along(green, "energy", -offset)
        total = total + jnp.sum(jnp.where(offsets == offset, weights, jnp.zeros_like(weights))) * partner
    return (green[None, None], total[None, None])


def solution(mesh):
    placed = (
        P("space", None, None, None),
        P("space", None, None, None),
        P("energy"),
        P("energy"),
        P("energy"),
        P("energy", None),
        P("energy", None),
    )
    return jax.shard_map(
        per_device,
        mesh=mesh,
        in_specs=placed,
        out_specs=(P("energy", "space", None, None, None), P("energy", "space", None, None, None)),
        check_vma=False,
    )
```

time: 1170 us -> 250 us (0.21); the launches traced: 1140 us -> 246 us
  other arithmetic: 769 us -> 14.3 us
  matrix products: 132 us -> 2.39 us
  local copies, waits for them, and re-layouts: 105 us -> 9.07 us
  waiting for transfers between devices: 69.1 us -> 128 us
  Pallas kernels: 0 us -> 55.1 us
  starting transfers between devices: 47.4 us -> 21 us
    another operation x119 -> x3, other arithmetic: 743 us -> 3.4 us  [the longest x2 3.36 us: adjoint(): jnp.stack([jnp.swapaxes(x[..., 0, :, :], -1, -2), -jnp.swapaxes(x[..., 1,...]
    another operation x120 -> x0, matrix products: 79.8 us -> none  [the longest x36 41.5 us: complex_inverse(): factor = jnp.linalg.cholesky(system)]
    another operation x103 -> x0, local copies, waits for them, and re-layouts: 70.9 us -> none  [the longest x79 64.8 us: complex_inverse(): solved = jax.scipy.linalg.cho_solve((factor, True), target)]
    all_gather x0 -> x2, waiting for transfers between devices: none -> 62.1 us  [the longest x1 34.2 us: per_device(): hop = lax.all_gather(hopping[0], 'space')]
    pallas_call x0 -> x1, Pallas kernels: none -> 55.1 us  [green_blocks(): pl.pallas_call(green_kernel, out_shape=jax.ShapeDtypeStruct((2, N, N), f3...]
    dot_general x76 -> x4, matrix products: 52.5 us -> 2.39 us  [the longest x1 0.6 us: xproduct(): d(a[1], b[1])]
    ppermute x14 -> x8, starting transfers between devices: 47.4 us -> 20.9 us  [passed_along(): return lax.ppermute(array, axis, pairs)]
    unnamed x111 -> x10, local copies, waits for them, and re-layouts: 17.7 us -> 4.1 us
  transfers between devices with their start and end apart: 14 -> 10, of which waited for: 9 -> 8; matrix products, arithmetic and copies ran while one was open for 16% -> 4% of each run, Pallas kernels for 0% -> 0%
where the time goes in v1:
time: 250 us; the launch traced here: 246 us
  waiting for transfers between devices  128 us (51%)
  Pallas kernels  55.1 us (22%)
  starting transfers between devices  21 us (8%)
  between operations  16.2 us (6%)
  other arithmetic  14.3 us (6%)
  local copies, waits for them, and re-layouts  9.07 us (4%)
    ppermute x8, waiting for transfers between devices, passed_along(): return lax.ppermute(array, axis, pairs)  66.3 us
    pallas_call x1, Pallas kernels, green_blocks(): pl.pallas_call(green_kernel, out_shape=jax.ShapeDtypeStruct((2, N, N), f3...  55.1 us
    all_gather x1, waiting for transfers between devices, per_device(): hop = lax.all_gather(hopping[0], 'space')  34.2 us
    all_gather x1, waiting for transfers between devices, per_device(): ham = lax.all_gather(ham_blocks[0], 'space')  27.8 us
    ppermute x8, starting transfers between devices, passed_along(): return lax.ppermute(array, axis, pairs)  20.9 us
    broadcast_in_dim x1, other arithmetic, per_device(): return (green[None, None], total[None, None])  6.05 us
  transfers between devices with their start and end apart: 10, of which 8 were waited for; matrix products, arithmetic and copies ran while one was open for 4% of the time, Pallas kernels for 0%

profile of v1, /device:TPU:1, one launch (start us, length us, event | category | flops | bytes accessed | tf_op | source)
XLA Modules:
  0.0 246.4 jit_solution(11628539213579332108)
XLA Ops:
  7.2 2.0 copy.12
  9.3 2.0 copy.9
  13.3 0.1 pad_maximum_fusion.1.level_ref
  13.4 34.2 %all-gather.5.cloned.1.call-done = f32[4,2,256,256]{2,3,0,1:T(8,128)} async-done(((f32[1,2,256,256]{2,3,0,1:T(8,128)}), f32[4,2,256,256]{2,3,0,1:T(8,128)}) %all-gather.5.cloned.1.call-update) | async-done | bytes 2097168 | tf_op jit(solution)/shard_map/all_gather | solution.py:296
  47.6 3.0 %copy.14 = f32[4,2,256,256]{3,2,1,0:T(8,128)} copy(f32[4,2,256,256]{2,3,0,1:T(8,128)} %all-gather.5.cloned.1.call-done) | data formatting | bytes 4194304 | tf_op jit(solution)/shard_map/all_gather | solution.py:296
  50.7 0.3 slice_bitcast_fusion.1
  51.0 0.6 fusion.6
  51.6 0.6 fusion.1
  52.2 0.6 fusion.7
  52.8 0.6 fusion.2
  53.4 2.2 maximum_maximum_fusion.hop_ref
  55.6 27.8 %all-gather.3.cloned.1.call-done = f32[4,2,256,256]{2,3,0,1:T(8,128)} async-done(((f32[1,2,256,256]{2,3,0,1:T(8,128)}), f32[4,2,256,256]{2,3,0,1:T(8,128)}) %all-gather.3.cloned.1.call-update) | async-done | bytes 2097168 | tf_op jit(solution)/shard_map/all_gather | solution.py:295
  83.5 3.1 %slice_bitcast_fusion = (f32[4,1,256,256]{3,2,1,0:T(8,128)}, f32[4,1,256,256]{3,2,1,0:T(8,128)}) fusion(f32[4,2,256,256]{2,3,0,1:T(8,128)} %all-gather.3.cloned.1.call-done), kind=kLoop, calls=%fused_computation.10 | loop fusion | flops 262144 | bytes 4194304 | tf_op jit(solution)/shard_map/stack | solution.py:285
  86.6 1.9 copy.11
  88.5 1.8 fusion.herm_ref
  90.4 55.1 %shard_map.86 = f32[2,256,256]{2,1,0:T(8,128)} custom-call(s32[1]{0:T(128)} %bitcast.place_ref, f32[3]{0:T(128)S(1)} %pad_maximum_fusion.1.level_ref, f32[4,2,256,256]{3,2,1,0:T(8,128)S(1)} %fusion.herm_ref, f32[2,256,256]{2,1,0:T(8,128)S(1)} %pad_maximum_fusion.gram_ref, f32[8,2,256,256]{3,2,1,0:T(8,128)} %maximum_maximum_fusion.hop_ref), custom_call_target="tpu_custom_call" | custom-call | flops 10000000000 | bytes 10000000 | tf_op jit(solution)/shard_map/pallas_call | solution.py:273
  145.5 4.2 %collective-permute-start = (f32[2,256,256]{2,1,0:T(8,128)}, f32[2,256,256]{2,1,0:T(8,128)S(1)}, u32[]{:S(2)}, u32[]{:S(2)}) collective-permute-start(f32[2,256,256]{2,1,0:T(8,128)} %shard_map.86), channel_id=1, source_target_pairs={{0,4},{1,5},{2,6},{3,7},{4,8},{5,9},{6,10},{7,11},{8,12},{9,13},{1... | collective-permute-start | bytes 1572872 | tf_op jit(solution)/shard_map/ppermute | solution.py:22
  149.7 6.2 %collective-permute-start.1 = (f32[2,256,256]{2,1,0:T(8,128)}, f32[2,256,256]{2,1,0:T(8,128)S(1)}, u32[]{:S(2)}, u32[]{:S(2)}) collective-permute-start(f32[2,256,256]{2,1,0:T(8,128)} %shard_map.86), channel_id=1, source_target_pairs={{0,3},{1,4},{2,5},{3,6},{4,7},{5,8},{6,9},{7,10},{8,11},{9,12},{10... | collective-permute-start | bytes 1572872 | tf_op jit(solution)/shard_map/ppermute | solution.py:22
  155.9 2.3 collective-permute-start.2
  158.2 2.1 collective-permute-start.3
  160.3 2.3 collective-permute-start.4
  162.6 3.0 %collective-permute-done = f32[2,256,256]{2,1,0:T(8,128)S(1)} collective-permute-done((f32[2,256,256]{2,1,0:T(8,128)}, f32[2,256,256]{2,1,0:T(8,128)S(1)}, u32[]{:S(2)}, u32[]{:S(2)}) %collective-permute-start) | collective-permute-done | bytes 524320 | tf_op jit(solution)/shard_map/ppermute | solution.py:22
  165.6 1.3 collective-permute-start.5
  166.9 20.4 %collective-permute-done.1 = f32[2,256,256]{2,1,0:T(8,128)S(1)} collective-permute-done((f32[2,256,256]{2,1,0:T(8,128)}, f32[2,256,256]{2,1,0:T(8,128)S(1)}, u32[]{:S(2)}, u32[]{:S(2)}) %collective-permute-start.1) | collective-permute-done | bytes 524320 | tf_op jit(solution)/shard_map/ppermute | solution.py:22
  187.3 1.3 collective-permute-start.6
  188.6 11.6 %collective-permute-done.2 = f32[2,256,256]{2,1,0:T(8,128)S(1)} collective-permute-done((f32[2,256,256]{2,1,0:T(8,128)}, f32[2,256,256]{2,1,0:T(8,128)S(1)}, u32[]{:S(2)}, u32[]{:S(2)}) %collective-permute-start.2) | collective-permute-done | bytes 524320 | tf_op jit(solution)/shard_map/ppermute | solution.py:22
  200.1 1.3 collective-permute-start.7
  201.4 0.7 fusion.8
  202.2 4.8 %collective-permute-done.3 = f32[2,256,256]{2,1,0:T(8,128)S(1)} collective-permute-done((f32[2,256,256]{2,1,0:T(8,128)}, f32[2,256,256]{2,1,0:T(8,128)S(1)}, u32[]{:S(2)}, u32[]{:S(2)}) %collective-permute-start.3) | collective-permute-done | bytes 524320 | tf_op jit(solution)/shard_map/ppermute | solution.py:22
  206.9 19.3 %collective-permute-done.6 = f32[2,256,256]{2,1,0:T(8,128)S(1)} collective-permute-done((f32[2,256,256]{2,1,0:T(8,128)}, f32[2,256,256]{2,1,0:T(8,128)S(1)}, u32[]{:S(2)}, u32[]{:S(2)}) %collective-permute-start.6) | collective-permute-done | bytes 524320 | tf_op jit(solution)/shard_map/ppermute | solution.py:22
  226.2 7.3 %collective-permute-done.7 = f32[2,256,256]{2,1,0:T(8,128)S(1)} collective-permute-done((f32[2,256,256]{2,1,0:T(8,128)}, f32[2,256,256]{2,1,0:T(8,128)S(1)}, u32[]{:S(2)}, u32[]{:S(2)}) %collective-permute-start.7) | collective-permute-done | bytes 524320 | tf_op jit(solution)/shard_map/ppermute | solution.py:22
  233.5 6.0 %add_bitcast_fusion = f32[1,1,2,256,256]{4,3,2,1,0:T(8,128)} fusion(f32[2,256,256]{2,1,0:T(8,128)S(1)} %collective-permute-done.7, f32[2,256,256]{2,1,0:T(8,128)S(1)} %collective-permute-done.6, f32[2,256,256]{2,1,0:T(8,128)S(1)} %collective-permute-done.5, f32[2,256,256]{2,1,0:T(8,128)S(1)} %collective-permute-done.4, ...), kind=kLoop, calls=%fused_computation.16 | loop fusion | flops 1966080 | bytes 4718624 | tf_op jit(solution)/shard_map/broadcast_in_dim | solution.py:308
  (15 shorter events, 0.2 us)
Async XLA Ops:
  7.2 40.5 %all-gather.5.cloned.1.call-start = ((), (), s32[]{:S(2)}) async-start(), calls=%async_computation.1 | async-start | bytes 2621440 | tf_op jit(solution)/shard_map/all_gather | solution.py:296
  9.3 74.2 %all-gather.3.cloned.1.call-start = ((), (), s32[]{:S(2)}) async-start(), calls=%async_computation | async-start | bytes 2621440 | tf_op jit(solution)/shard_map/all_gather | solution.py:295
  47.6 3.0 %copy-start = (f32[4,2,256,256]{2,3,0,1:T(8,128)S(1)}, f32[4,2,256,256]{2,3,0,1:T(8,128)}, u32[]{:S(2)}) copy-start(f32[4,2,256,256]{2,3,0,1:T(8,128)} %all-gather.5.cloned.1.call-done) | copy-start | bytes 6291460
  51.6 1.9 copy-start.1
  90.4 111.1 %copy-start.2 = (f32[1,8]{1,0:T(1,128)S(1)}, f32[1,8]{1,0:T(1,128)}, u32[]{:S(2)}) copy-start(f32[1,8]{1,0:T(1,128)} %param.13) | copy-start | bytes 100
  90.4 111.1 %copy-start.3 = (s32[1,8]{1,0:T(1,128)S(1)}, s32[1,8]{1,0:T(1,128)}, u32[]{:S(2)}) copy-start(s32[1,8]{1,0:T(1,128)} %param.12) | copy-start | bytes 100
  145.5 20.1 %collective-permute-start = (f32[2,256,256]{2,1,0:T(8,128)}, f32[2,256,256]{2,1,0:T(8,128)S(1)}, u32[]{:S(2)}, u32[]{:S(2)}) collective-permute-start(f32[2,256,256]{2,1,0:T(8,128)} %shard_map.86), channel_id=1, source_target_pairs={{0,4},{1,5},{2,6},{3,7},{4,8},{5,9},{6,10},{7,11},{8,12},{9,13},{1... | collective-permute-start | bytes 1572872 | tf_op jit(solution)/shard_map/ppermute | solution.py:22
  149.7 37.6 %collective-permute-start.1 = (f32[2,256,256]{2,1,0:T(8,128)}, f32[2,256,256]{2,1,0:T(8,128)S(1)}, u32[]{:S(2)}, u32[]{:S(2)}) collective-permute-start(f32[2,256,256]{2,1,0:T(8,128)} %shard_map.86), channel_id=1, source_target_pairs={{0,3},{1,4},{2,5},{3,6},{4,7},{5,8},{6,9},{7,10},{8,11},{9,12},{10... | collective-permute-start | bytes 1572872 | tf_op jit(solution)/shard_map/ppermute | solution.py:22
  155.9 44.2 %collective-permute-start.2 = (f32[2,256,256]{2,1,0:T(8,128)}, f32[2,256,256]{2,1,0:T(8,128)S(1)}, u32[]{:S(2)}, u32[]{:S(2)}) collective-permute-start(f32[2,256,256]{2,1,0:T(8,128)} %shard_map.86), channel_id=1, source_target_pairs={{0,2},{1,3},{2,4},{3,5},{4,6},{5,7},{6,8},{7,9},{8,10},{9,11},{10,... | collective-permute-start | bytes 1572872 | tf_op jit(solution)/shard_map/ppermute | solution.py:22
  158.2 48.7 %collective-permute-start.3 = (f32[2,256,256]{2,1,0:T(8,128)}, f32[2,256,256]{2,1,0:T(8,128)S(1)}, u32[]{:S(2)}, u32[]{:S(2)}) collective-permute-start(f32[2,256,256]{2,1,0:T(8,128)} %shard_map.86), channel_id=1, source_target_pairs={{0,1},{1,2},{2,3},{3,4},{4,5},{5,6},{6,7},{7,8},{8,9},{9,10},{10,1... | collective-permute-start | bytes 1572872 | tf_op jit(solution)/shard_map/ppermute | solution.py:22
  160.3 46.6 %collective-permute-start.4 = (f32[2,256,256]{2,1,0:T(8,128)}, f32[2,256,256]{2,1,0:T(8,128)S(1)}, u32[]{:S(2)}, u32[]{:S(2)}) collective-permute-start(f32[2,256,256]{2,1,0:T(8,128)} %shard_map.86), channel_id=1, source_target_pairs={{1,0},{2,1},{3,2},{4,3},{5,4},{6,5},{7,6},{8,7},{9,8},{10,9},{11,1... | collective-permute-start | bytes 1572872 | tf_op jit(solution)/shard_map/ppermute | solution.py:22
  165.6 41.3 %collective-permute-start.5 = (f32[2,256,256]{2,1,0:T(8,128)}, f32[2,256,256]{2,1,0:T(8,128)S(1)}, u32[]{:S(2)}, u32[]{:S(2)}) collective-permute-start(f32[2,256,256]{2,1,0:T(8,128)} %shard_map.86), channel_id=1, source_target_pairs={{2,0},{3,1},{4,2},{5,3},{6,4},{7,5},{8,6},{9,7},{10,8},{11,9},{12,... | collective-permute-start | bytes 1572872 | tf_op jit(solution)/shard_map/ppermute | solution.py:22
  187.3 38.9 %collective-permute-start.6 = (f32[2,256,256]{2,1,0:T(8,128)}, f32[2,256,256]{2,1,0:T(8,128)S(1)}, u32[]{:S(2)}, u32[]{:S(2)}) collective-permute-start(f32[2,256,256]{2,1,0:T(8,128)} %shard_map.86), channel_id=1, source_target_pairs={{3,0},{4,1},{5,2},{6,3},{7,4},{8,5},{9,6},{10,7},{11,8},{12,9},{13... | collective-permute-start | bytes 1572872 | tf_op jit(solution)/shard_map/ppermute | solution.py:22
  200.1 33.4 %collective-permute-start.7 = (f32[2,256,256]{2,1,0:T(8,128)}, f32[2,256,256]{2,1,0:T(8,128)S(1)}, u32[]{:S(2)}, u32[]{:S(2)}) collective-permute-start(f32[2,256,256]{2,1,0:T(8,128)} %shard_map.86), channel_id=1, source_target_pairs={{4,0},{5,1},{6,2},{7,3},{8,4},{9,5},{10,6},{11,7},{12,8},{13,9},{1... | collective-permute-start | bytes 1572872 | tf_op jit(solution)/shard_map/ppermute | solution.py:22
Sparse Core Ops, SparseCore 0:
  10.4 37.2 all-gather.4
  50.0 33.4 all-gather.2

commit v2 on v1

--- a/solution.py
+++ b/solution.py
@@ -7,7 +7,6 @@
 from jax.experimental.pallas import tpu as pltpu
 from jax.sharding import PartitionSpec as P
 
-SHIFT = 4
 N = 256
 SUB = 32
 f32 = jnp.float32
@@ -16,10 +15,177 @@
 SLOTS = 256
 
 
-def passed_along(array, axis, by):
-    peers = lax.axis_size(axis)
-    pairs = [(i, i + by) for i in range(peers) if 0 <= i + by < peers]
-    return lax.ppermute(array, axis, pairs)
+CHUNKS = 4
+PIECE = 512 // CHUNKS
+MESH = pl.DeviceIdType.MESH
+
+
+def greet(partners):
+    barrier = pltpu.get_barrier_semaphore()
+    for partner in partners:
+        pl.semaphore_signal(barrier, inc=1, device_id=partner, device_id_type=MESH)
+    pl.semaphore_wait(barrier, len(partners))
+
+
+def gather_kernel(ham_ref, hop_ref, out_ref, herm, local_sem, send_sem, recv_sem):
+    places = lax.axis_size("space")
+    me = lax.axis_index("space")
+    point = lax.axis_index("energy")
+    core = lax.rem(point, 2)
+    up, down = lax.rem(me + 1, places), lax.rem(me + places - 1, places)
+    across = lax.rem(me + 2, places)
+    above, below, beside = {"space": up}, {"space": down}, {"energy": point + 1 - 2 * core}
+    greet((above, below, beside))
+    rows = pl.ds(pl.multiple_of(128 * core, 128), 128)
+    HERM, HOP = pl.ds(0, 2), pl.ds(2, 2)
+    started = []
+
+    def send(source, block, part, to, slot):
+        copy = pltpu.make_async_remote_copy(
+            src_ref=source,
+            dst_ref=out_ref.at[block, part, rows],
+            send_sem=send_sem.at[slot],
+            recv_sem=recv_sem.at[slot],
+            device_id=to,
+            device_id_type=MESH,
+        )
+        copy.start()
+        started.append(copy)
+        return copy
+
+    def pass_on(block, part, to, slot):
+        return send(out_ref.at[block, part, rows], block, part, to, slot)
+
+    hop_up = send(hop_ref.at[:, rows], me, HOP, above, 0)
+    hop_down = send(hop_ref.at[:, rows], me, HOP, below, 1)
+    herm[0] = 0.5 * (ham_ref[0] + ham_ref[0].T)
+    herm[1] = 0.5 * (ham_ref[1] - ham_ref[1].T)
+    herm_down = send(herm.at[:, rows], me, HERM, below, 2)
+    herm_up = send(herm.at[:, rows], me, HERM, above, 3)
+    own = [
+        pltpu.make_async_copy(herm, out_ref.at[me, HERM], local_sem.at[0]),
+        pltpu.make_async_copy(hop_ref, out_ref.at[me, HOP], local_sem.at[1]),
+    ]
+    for copy in own:
+        copy.start()
+    hop_up.wait_recv()
+    hop_far = pass_on(down, HOP, above, 4)
+    swaps = [pass_on(down, HOP, beside, 6)]
+    hop_down.wait_recv()
+    swaps.append(pass_on(up, HOP, beside, 7))
+    herm_down.wait_recv()
+    herm_far = pass_on(up, HERM, below, 5)
+    swaps.append(pass_on(up, HERM, beside, 8))
+    herm_up.wait_recv()
+    swaps.append(pass_on(down, HERM, beside, 9))
+    hop_far.wait_recv()
+    swaps.append(pass_on(across, HOP, beside, 10))
+    herm_far.wait_recv()
+    swaps.append(pass_on(across, HERM, beside, 11))
+    for copy in swaps:
+        copy.wait_recv()
+    for copy in started:
+        copy.wait_send()
+    for copy in own:
+        copy.wait()
+
+
+def gathered(ham, hop):
+    vmem = pl.BlockSpec(memory_space=pltpu.VMEM)
+    return pl.pallas_call(
+        gather_kernel,
+        out_shape=jax.ShapeDtypeStruct((4, 4, N, N), f32),
+        in_specs=[vmem, vmem],
+        out_specs=pl.BlockSpec(memory_space=pl.ANY),
+        scratch_shapes=[
+            pltpu.VMEM((2, N, N), f32),
+            pltpu.SemaphoreType.DMA((2,)),
+            pltpu.SemaphoreType.DMA((12,)),
+            pltpu.SemaphoreType.DMA((12,)),
+        ],
+        compiler_params=pltpu.CompilerParams(collective_id=0, has_side_effects=True, vmem_limit_bytes=16 << 20),
+        cost_estimate=pl.CostEstimate(flops=10**6, bytes_accessed=10**7, transcendentals=0),
+    )(ham, hop)
+
+
+def phonon_kernel(weight_ref, green_ref, out_ref, near, far, side, send_sem, recv_sem):
+    points = lax.axis_size("energy")
+    point = lax.axis_index("energy")
+    core = lax.rem(point, 2)
+    after, before = {"energy": lax.rem(point + 2, points)}, {"energy": lax.rem(point + points - 2, points)}
+    beside = {"energy": point + 1 - 2 * core}
+    along = (after, before)
+    greet((after, before, beside))
+    started = []
+
+    def piece(i):
+        return pl.ds(PIECE * i, PIECE)
+
+    def send(source, target, to, slot):
+        copy = pltpu.make_async_remote_copy(
+            src_ref=source,
+            dst_ref=target,
+            send_sem=send_sem.at[slot],
+            recv_sem=recv_sem.at[slot],
+            device_id=to,
+            device_id_type=MESH,
+        )
+        copy.start()
+        started.append(copy)
+        return copy
+
+    def add(i, terms):
+        total = out_ref[piece(i)]
+        for k, ref in terms:
+            total = total + weight_ref[k] * ref[piece(i)]
+        out_ref[piece(i)] = total
+
+    first, second, swap = {}, {}, {}
+    for i in range(CHUNKS):
+        for d in range(2):
+            first[d, i] = send(green_ref.at[piece(i)], near.at[d, piece(i)], along[d], d * CHUNKS + i)
+    for i in range(CHUNKS):
+        swap[0, i] = send(green_ref.at[piece(i)], side.at[0, piece(i)], beside, 4 * CHUNKS + i)
+    for i in range(CHUNKS):
+        for d in range(2):
+            first[d, i].wait_recv()
+            second[d, i] = send(near.at[d, piece(i)], far.at[d, piece(i)], along[d], (2 + d) * CHUNKS + i)
+            swap[1 + d, i] = send(near.at[d, piece(i)], side.at[1 + d, piece(i)], beside, (5 + d) * CHUNKS + i)
+        swap[0, i].wait_recv()
+        out_ref[piece(i)] = weight_ref[4] * side[0, piece(i)]
+        add(i, [(0, near.at[0]), (1, near.at[1])])
+    for i in range(CHUNKS):
+        second[0, i].wait_recv()
+        second[1, i].wait_recv()
+        swap[3, i] = send(far.at[1 - core, piece(i)], side.at[3, piece(i)], beside, 7 * CHUNKS + i)
+        swap[1, i].wait_recv()
+        swap[2, i].wait_recv()
+        add(i, [(2, far.at[0]), (3, far.at[1]), (5, side.at[1]), (6, side.at[2])])
+    for i in range(CHUNKS):
+        swap[3, i].wait_recv()
+        add(i, [(7, side.at[3])])
+    for copy in started:
+        copy.wait_send()
+
+
+def phonon_sum(weights, green):
+    vmem = pl.BlockSpec(memory_space=pltpu.VMEM)
+    block = (512, N)
+    return pl.pallas_call(
+        phonon_kernel,
+        out_shape=jax.ShapeDtypeStruct(block, f32),
+        in_specs=[pl.BlockSpec(memory_space=pltpu.SMEM), vmem],
+        out_specs=vmem,
+        scratch_shapes=[
+            pltpu.VMEM((2, *block), f32),
+            pltpu.VMEM((2, *block), f32),
+            pltpu.VMEM((4, *block), f32),
+            pltpu.SemaphoreType.DMA((8 * CHUNKS,)),
+            pltpu.SemaphoreType.DMA((8 * CHUNKS,)),
+        ],
+        compiler_params=pltpu.CompilerParams(collective_id=1, has_side_effects=True, vmem_limit_bytes=24 << 20),
+        cost_estimate=pl.CostEstimate(flops=10**6, bytes_accessed=10**7, transcendentals=0),
+    )(weights, green)
 
 
 def cmul(a, b):
@@ -220,36 +386,55 @@
     re[...], im[...] = x
 
 
-def green_kernel(place_ref, level_ref, herm_ref, gram_ref, hop_ref, out_ref, outer, work, near, side_term, scr):
+def green_kernel(place_ref, level_ref, all_ref, out_ref, outer, work, near, side_term, lefts, scr):
     rows_of = Rows(scr)
     place = place_ref[0]
     side = place // 2
     e, eta, c = level_ref[0], level_ref[1], level_ref[2]
     eye = (lax.broadcasted_iota(jnp.int32, (N, N), 0) == lax.broadcasted_iota(jnp.int32, (N, N), 1)).astype(f32)
-    near_l, near_r = jnp.where(side == 0, 5, 3), jnp.where(side == 0, 1, 7)
-    far_l, far_r = jnp.where(side == 0, 3, 5), jnp.where(side == 0, 7, 1)
-    mid_l, mid_r = jnp.where(side == 0, 2, 6), jnp.where(side == 0, 6, 2)
-
-    put(planes(outer.at[0]), (e * eye - herm_ref[0, 0] - c * gram_ref[1], eta * eye - herm_ref[0, 1] + c * gram_ref[0]))
-    put(planes(outer.at[1]), (e * eye - herm_ref[3, 0], (eta + c) * eye - herm_ref[3, 1]))
+    herm = lambda k: (all_ref[k, 0], all_ref[k, 1])
+    hop = lambda k: (all_ref[k, 2], all_ref[k, 3])
+    back = lambda k: (all_ref[k, 2].T, -all_ref[k, 3].T)
+
+    gram = product(hop(0), back(0))
+    h0, h3 = herm(0), herm(3)
+    put(planes(outer.at[0]), (e * eye - h0[0] - c * gram[1], eta * eye - h0[1] + c * gram[0]))
+    put(planes(outer.at[1]), (e * eye - h3[0], (eta + c) * eye - h3[1]))
+    put(planes(lefts.at[0]), back(1))
+    put(planes(lefts.at[1]), hop(1))
+    put(planes(lefts.at[2]), hop(3))
+    put(planes(lefts.at[3]), back(3))
+
+    @pl.when(side == 0)
+    def _():
+        put(planes(lefts.at[4]), hop(2))
+        put(planes(lefts.at[5]), back(2))
+
+    @pl.when(side == 1)
+    def _():
+        put(planes(lefts.at[4]), back(2))
+        put(planes(lefts.at[5]), hop(2))
+
     invert([planes(outer.at[0]), planes(outer.at[1])], rows_of)
 
     def inner(i, sigma):
-        return (e * eye - herm_ref[i, 0] - sigma[0], eta * eye - herm_ref[i, 1] - sigma[1])
-
-    right = product(pair(outer.at[side]), pair(hop_ref.at[near_r]))
+        h = herm(i)
+        return (e * eye - h[0] - sigma[0], eta * eye - h[1] - sigma[1])
+
+    far = 1 - side
+    right = product(pair(outer.at[far]), pair(lefts.at[2 * far + 1]))
+    put(work, inner(1 + far, product(pair(lefts.at[2 * far]), right)))
+    right = product(pair(outer.at[side]), pair(lefts.at[2 * side + 1]))
     put(side_term, right)
-    put(near, inner(1 + side, product(pair(hop_ref.at[near_l]), right)))
-    right = product(pair(outer.at[1 - side]), pair(hop_ref.at[far_r]))
-    put(work, inner(2 - side, product(pair(hop_ref.at[far_l]), right)))
+    put(near, inner(1 + side, product(pair(lefts.at[2 * side]), right)))
 
     def solve(step, carry):
         invert([planes(work)], rows_of)
 
         @pl.when(step == 0)
         def _():
-            right = product(pair(work), pair(hop_ref.at[mid_r]))
-            put(work, csub(pair(near), product(pair(hop_ref.at[mid_l]), right)))
+            right = product(pair(work), pair(lefts.at[5]))
+            put(work, csub(pair(near), product(pair(lefts.at[4]), right)))
 
         return carry
 
@@ -262,49 +447,44 @@
     @pl.when((place == 0) | (place == 3))
     def _():
         own = pair(outer.at[side])
-        left = product(pair(hop_ref.at[near_l]), own)
+        left = product(pair(lefts.at[2 * side]), own)
         put(out_ref, cadd(own, product(pair(side_term), product(pair(work), left))))
 
 
-def green_blocks(place, levels, herm, gram, hops):
+def green_block(place, levels, everything):
     vmem = pl.BlockSpec(memory_space=pltpu.VMEM)
     smem = pl.BlockSpec(memory_space=pltpu.SMEM)
     block = pltpu.VMEM((2, N, N), f32)
     return pl.pallas_call(
         green_kernel,
         out_shape=jax.ShapeDtypeStruct((2, N, N), f32),
-        in_specs=[smem, smem, vmem, vmem, vmem],
+        in_specs=[smem, smem, vmem],
         out_specs=vmem,
-        scratch_shapes=[pltpu.VMEM((2, 2, N, N), f32), block, block, block, pltpu.VMEM((8 * SLOTS, 128), f32)],
+        scratch_shapes=[
+            pltpu.VMEM((2, 2, N, N), f32),
+            block,
+            block,
+            block,
+            pltpu.VMEM((6, 2, N, N), f32),
+            pltpu.VMEM((8 * SLOTS, 128), f32),
+        ],
         compiler_params=pltpu.CompilerParams(vmem_limit_bytes=48 << 20),
         cost_estimate=pl.CostEstimate(flops=10**10, bytes_accessed=10**7, transcendentals=0),
-    )(place, levels, herm, gram, hops)
-
-
-def adjoint(x):
-    return jnp.stack([jnp.swapaxes(x[..., 0, :, :], -1, -2), -jnp.swapaxes(x[..., 1, :, :], -1, -2)], -3)
-
-
-def xproduct(a, b):
-    d = functools.partial(jnp.dot, precision=lax.Precision.HIGHEST)
-    return jnp.stack([d(a[0], b[0]) - d(a[1], b[1]), d(a[0], b[1]) + d(a[1], b[0])])
+    )(place, levels, everything)
 
 
 def per_device(ham_blocks, hopping, energy, broadening, contact, phonon_offset, phonon_weight):
     place = lax.axis_index("space").astype(jnp.int32).reshape(1)
-    ham = lax.all_gather(ham_blocks[0], "space")
-    hop = lax.all_gather(hopping[0], "space")
-    herm = 0.5 * (ham + adjoint(ham))
-    hops = jnp.concatenate([hop, adjoint(hop)], 0)
-    gram = xproduct(hops[0], hops[4])
-    levels = jnp.concatenate([energy, broadening, contact])
-    green = green_blocks(place, levels, herm, gram, hops)
-    offsets = phonon_offset[0]
-    weights = phonon_weight[0]
-    total = jnp.zeros_like(green)
-    for offset in list(range(-SHIFT, 0)) + list(range(1, SHIFT + 1)):
-        partner = passed_along(green, "energy", -offset)
-        total = total + jnp.sum(jnp.where(offsets == offset, weights, jnp.zeros_like(weights))) * partner
+    point = lax.axis_index("energy").astype(jnp.int32)
+    points = lax.axis_size("energy")
+    everything = gathered(ham_blocks[0], hopping[0])
+    green = green_block(place, jnp.concatenate([energy, broadening, contact]), everything)
+    offsets, weights = phonon_offset[0], phonon_weight[0]
+    inside = (point + offsets >= 0) & (point + offsets < points)
+    even = point % 2 == 0
+    reach = [-2, 2, -4, 4] + [jnp.where(even, a, b) for a, b in ((1, -1), (-1, -3), (3, 1), (-3, 3))]
+    weight_of = jnp.stack([jnp.sum(jnp.where(inside & (offsets == d), weights, 0.0)) for d in reach])
+    total = phonon_sum(weight_of, green.reshape(512, N)).reshape(2, N, N)
     return (green[None, None], total[None, None])
 
 

time: 250 us -> 126 us (0.50); the launches traced: 246 us -> 126 us
  waiting for transfers between devices: 128 us -> 0 us
  Pallas kernels: 55.1 us -> 113 us
  starting transfers between devices: 21 us -> 0 us
  between operations: 16.2 us -> 2.61 us
  other arithmetic: 14.3 us -> 1.45 us
    ppermute x8 -> x0, waiting for transfers between devices: 66.3 us -> none  [passed_along(): return lax.ppermute(array, axis, pairs)]
    all_gather x2 -> x0, waiting for transfers between devices: 62.1 us -> none  [the longest x1 34.2 us: per_device(): hop = lax.all_gather(hopping[0], 'space')]
    pallas_call x1 -> x3, Pallas kernels: 55.1 us -> 113 us  [the longest x1 54.1 us: green_block(): pl.pallas_call(green_kernel, out_shape=jax.ShapeDtypeStruct((2, N, N), f3...]
    ppermute x8 -> x0, starting transfers between devices: 20.9 us -> none  [passed_along(): return lax.ppermute(array, axis, pairs)]
    broadcast_in_dim x1 -> x0, other arithmetic: 6.05 us -> none  [per_device(): return (green[None, None], total[None, None])]
    another operation x0 -> x1, local copies, waits for them, and re-layouts: none -> 5.02 us  [per_device(): jnp.stack([jnp.sum(jnp.where(inside & (offsets == d), weights, 0.0)) for...]
    all_gather x2 -> x0, local copies, waits for them, and re-layouts: 4.97 us -> none  [the longest x1 3.05 us: per_device(): hop = lax.all_gather(hopping[0], 'space')]
    another operation x3 -> x0, other arithmetic: 3.4 us -> none  [the longest x2 3.36 us: adjoint(): jnp.stack([jnp.swapaxes(x[..., 0, :, :], -1, -2), -jnp.swapaxes(x[..., 1,...]
  transfers between devices with their start and end apart: 10 -> 0, of which waited for: 8 -> 0; matrix products, arithmetic and copies ran while one was open for 4% -> 0% of each run, Pallas kernels for 0% -> 0%
where the time goes in v2:
time: 126 us
  Pallas kernels  113 us (90%)
  local copies, waits for them, and re-layouts  8.94 us (7%)
  between operations  2.61 us (2%)
  other arithmetic  1.45 us (1%)
    pallas_call x1, Pallas kernels, green_block(): pl.pallas_call(green_kernel, out_shape=jax.ShapeDtypeStruct((2, N, N), f3...  54.1 us
    pallas_call x1, Pallas kernels, phonon_sum(): pl.pallas_call(phonon_kernel, out_shape=jax.ShapeDtypeStruct(block, f32),...  34.6 us
    pallas_call x1, Pallas kernels, gathered(): pl.pallas_call(gather_kernel, out_shape=jax.ShapeDtypeStruct((4, 4, N, N)...  24.4 us
    another operation x1, local copies, waits for them, and re-layouts, per_device(): jnp.stack([jnp.sum(jnp.where(inside & (offsets == d), weights, 0.0)) for...  5.02 us
    unnamed x7, local copies, waits for them, and re-layouts  3.92 us

profile of v2, /device:TPU:1, one launch (start us, length us, event | category | flops | bytes accessed | tf_op | source)
XLA Modules:
  0.0 126.1 jit_solution(640845903444254841)
XLA Ops:
  2.6 0.1 pad_maximum_fusion.level_ref
  2.7 1.4 %fusion.7 = (f32[]{:T(128)}, f32[]{:T(128)}, f32[]{:T(128)}, f32[]{:T(128)}, f32[]{:T(128)}, /*index=5*/f32[]{:T(128)}, f32[]{:T(128)}, f32[]{:T(128)}) fusion(f32[1,8]{1,0:T(1,128)} %param.13, s32[1,8]{1,0:T(1,128)} %param.12, s32[]{:T(128)S(6)} %select_n.56, s32[]{:T(128)S(6)} %axis_index.25, s32[]{:T(128)S(6)} %select_n.54, s32[]{:T(128)S(6)} %select_n.52, ...), kind=kLoop, calls=%fused_computation.17 | loop fusion | flops 280 | bytes 116 | tf_op jit(solution)/shard_map/reduce_sum | solution.py:486
  4.0 5.0 %stack.35.weight_ref = f32[8]{0:T(128)S(1)} concatenate(f32[1]{0:T(128)} %bitcast.4, f32[1]{0:T(128)} %bitcast.5, f32[1]{0:T(128)} %bitcast.6, f32[1]{0:T(128)} %bitcast.7, f32[1]{0:T(128)} %bitcast.8, f32[1]{0:T(128)} %bitcast.9, f32[1]{0:T(128)} %bitcast.10, f32[1]{0:T(128)} %bitcast.11), dimensions={0} | concatenate | bytes 64 | tf_op jit(solution)/shard_map/stack | solution.py:486
  9.1 0.0 copy-start
  9.1 1.0 copy-done
  10.1 0.0 copy-start.1
  10.1 1.0 copy-done.1
  11.1 24.4 %shard_map.86.all_ref = f32[4,4,256,256]{3,2,1,0:T(8,128)S(1)} custom-call(f32[2,256,256]{2,1,0:T(8,128)S(1)} %bitcast.15, f32[2,256,256]{2,1,0:T(8,128)S(1)} %bitcast.16), custom_call_target="tpu_custom_call" | custom-call | flops 1000000 | bytes 10000000 | tf_op jit(solution)/shard_map/pallas_call | solution.py:95
  35.5 54.1 %shard_map.87 = f32[2,256,256]{2,1,0:T(8,128)} custom-call(s32[1]{0:T(128)} %bitcast.place_ref, f32[3]{0:T(128)S(1)} %pad_maximum_fusion.level_ref, f32[4,4,256,256]{3,2,1,0:T(8,128)S(1)} %shard_map.86.all_ref), custom_call_target="tpu_custom_call" | custom-call | flops 10000000000 | bytes 10000000 | tf_op jit(solution)/shard_map/pallas_call | solution.py:458
  89.6 0.0 copy-start.2
  89.6 1.0 copy-done.2
  90.7 34.6 %shard_map.88 = f32[512,256]{1,0:T(8,128)S(1)} custom-call(f32[8]{0:T(128)S(1)} %stack.35.weight_ref, f32[512,256]{1,0:T(8,128)S(1)} %bitcast.18), custom_call_target="tpu_custom_call" | custom-call | flops 1000000 | bytes 10000000 | tf_op jit(solution)/shard_map/pallas_call | solution.py:174
  125.3 0.8 copy.13
Async XLA Ops:
  9.1 1.0 copy-start
  10.1 1.0 copy-start.1
  89.6 1.0 copy-start.2

commit v3 on v2

--- a/solution.py
+++ b/solution.py
@@ -15,7 +15,7 @@
 SLOTS = 256
 
 
-CHUNKS = 4
+CHUNKS = 8
 PIECE = 512 // CHUNKS
 MESH = pl.DeviceIdType.MESH
 
@@ -27,7 +27,13 @@
     pl.semaphore_wait(barrier, len(partners))
 
 
-def gather_kernel(ham_ref, hop_ref, out_ref, herm, local_sem, send_sem, recv_sem):
+def triangles():
+    row = lax.broadcasted_iota(jnp.int32, (N, N), 0)
+    column = lax.broadcasted_iota(jnp.int32, (N, N), 1)
+    return row, column
+
+
+def gather_kernel(ham_ref, hop_ref, herms_ref, hops_ref, ham, herm, local_sem, send_sem, recv_sem):
     places = lax.axis_size("space")
     me = lax.axis_index("space")
     point = lax.axis_index("energy")
@@ -35,15 +41,20 @@
     up, down = lax.rem(me + 1, places), lax.rem(me + places - 1, places)
     across = lax.rem(me + 2, places)
     above, below, beside = {"space": up}, {"space": down}, {"energy": point + 1 - 2 * core}
+    fetch = pltpu.make_async_copy(ham_ref, ham, local_sem.at[0])
+    fetch.start()
+    own = [pltpu.make_async_copy(hop_ref, hops_ref.at[me], local_sem.at[1])]
+    own[0].start()
     greet((above, below, beside))
     rows = pl.ds(pl.multiple_of(128 * core, 128), 128)
-    HERM, HOP = pl.ds(0, 2), pl.ds(2, 2)
     started = []
-
-    def send(source, block, part, to, slot):
+    herms_of = lambda k: herms_ref.at[k, rows]
+    hops_of = lambda k, i: hops_ref.at[k, i, rows]
+
+    def send(source, target, to, slot):
         copy = pltpu.make_async_remote_copy(
             src_ref=source,
-            dst_ref=out_ref.at[block, part, rows],
+            dst_ref=target,
             send_sem=send_sem.at[slot],
             recv_sem=recv_sem.at[slot],
             device_id=to,
@@ -53,35 +64,42 @@
         started.append(copy)
         return copy
 
-    def pass_on(block, part, to, slot):
-        return send(out_ref.at[block, part, rows], block, part, to, slot)
-
-    hop_up = send(hop_ref.at[:, rows], me, HOP, above, 0)
-    hop_down = send(hop_ref.at[:, rows], me, HOP, below, 1)
-    herm[0] = 0.5 * (ham_ref[0] + ham_ref[0].T)
-    herm[1] = 0.5 * (ham_ref[1] - ham_ref[1].T)
-    herm_down = send(herm.at[:, rows], me, HERM, below, 2)
-    herm_up = send(herm.at[:, rows], me, HERM, above, 3)
-    own = [
-        pltpu.make_async_copy(herm, out_ref.at[me, HERM], local_sem.at[0]),
-        pltpu.make_async_copy(hop_ref, out_ref.at[me, HOP], local_sem.at[1]),
-    ]
-    for copy in own:
-        copy.start()
-    hop_up.wait_recv()
-    hop_far = pass_on(down, HOP, above, 4)
-    swaps = [pass_on(down, HOP, beside, 6)]
-    hop_down.wait_recv()
-    swaps.append(pass_on(up, HOP, beside, 7))
+    hop_up = [send(hop_ref.at[i, rows], hops_of(me, i), above, i) for i in (0, 1)]
+    hop_down = [send(hop_ref.at[i, rows], hops_of(me, i), below, 2 + i) for i in (1, 0)][::-1]
+    fetch.wait()
+    row, column = triangles()
+    herm[...] = 0.5 * jnp.where(row <= column, ham[0] + ham[0].T, ham[1] - ham[1].T)
+    herm_up = send(herm.at[rows], herms_of(me), above, 4)
+    herm_down = send(herm.at[rows], herms_of(me), below, 5)
+    own.append(pltpu.make_async_copy(herm, herms_ref.at[me], local_sem.at[2]))
+    own[1].start()
+    hop_up[0].wait_recv()
+    far_up = send(hops_of(down, 0), hops_of(down, 0), above, 6)
+    swaps = [send(hops_of(down, 0), hops_of(down, 0), beside, 9)]
+    hop_down[1].wait_recv()
+    far_down = send(hops_of(up, 1), hops_of(up, 1), below, 7)
+    swaps.append(send(hops_of(up, 1), hops_of(up, 1), beside, 10))
+    hop_up[1].wait_recv()
+    swaps.append(send(hops_of(down, 1), hops_of(down, 1), beside, 11))
+    hop_down[0].wait_recv()
+    swaps.append(send(hops_of(up, 0), hops_of(up, 0), beside, 12))
+    half = 64
+    top = pl.ds(pl.multiple_of(128 * core, 64), half)
+    bottom = pl.ds(pl.multiple_of(128 * core + half, 64), half)
+    herm_up.wait_recv()
+    far_top = send(herms_ref.at[down, top], herms_ref.at[down, top], above, 8)
+    swaps.append(send(herms_of(down), herms_of(down), beside, 13))
     herm_down.wait_recv()
-    herm_far = pass_on(up, HERM, below, 5)
-    swaps.append(pass_on(up, HERM, beside, 8))
-    herm_up.wait_recv()
-    swaps.append(pass_on(down, HERM, beside, 9))
-    hop_far.wait_recv()
-    swaps.append(pass_on(across, HOP, beside, 10))
-    herm_far.wait_recv()
-    swaps.append(pass_on(across, HERM, beside, 11))
+    far_bottom = send(herms_ref.at[up, bottom], herms_ref.at[up, bottom], below, 14)
+    swaps.append(send(herms_of(up), herms_of(up), beside, 15))
+    far_up.wait_recv()
+    swaps.append(send(hops_of(across, 0), hops_of(across, 0), beside, 16))
+    far_down.wait_recv()
+    swaps.append(send(hops_of(across, 1), hops_of(across, 1), beside, 17))
+    far_top.wait_recv()
+    swaps.append(send(herms_ref.at[across, top], herms_ref.at[across, top], beside, 18))
+    far_bottom.wait_recv()
+    swaps.append(send(herms_ref.at[across, bottom], herms_ref.at[across, bottom], beside, 19))
     for copy in swaps:
         copy.wait_recv()
     for copy in started:
@@ -91,17 +109,18 @@
 
 
 def gathered(ham, hop):
-    vmem = pl.BlockSpec(memory_space=pltpu.VMEM)
+    anywhere = pl.BlockSpec(memory_space=pl.ANY)
     return pl.pallas_call(
         gather_kernel,
-        out_shape=jax.ShapeDtypeStruct((4, 4, N, N), f32),
-        in_specs=[vmem, vmem],
-        out_specs=pl.BlockSpec(memory_space=pl.ANY),
+        out_shape=(jax.ShapeDtypeStruct((4, N, N), f32), jax.ShapeDtypeStruct((4, 2, N, N), f32)),
+        in_specs=[anywhere, anywhere],
+        out_specs=(anywhere, anywhere),
         scratch_shapes=[
             pltpu.VMEM((2, N, N), f32),
-            pltpu.SemaphoreType.DMA((2,)),
-            pltpu.SemaphoreType.DMA((12,)),
-            pltpu.SemaphoreType.DMA((12,)),
+            pltpu.VMEM((N, N), f32),
+            pltpu.SemaphoreType.DMA((3,)),
+            pltpu.SemaphoreType.DMA((20,)),
+            pltpu.SemaphoreType.DMA((20,)),
         ],
         compiler_params=pltpu.CompilerParams(collective_id=0, has_side_effects=True, vmem_limit_bytes=16 << 20),
         cost_estimate=pl.CostEstimate(flops=10**6, bytes_accessed=10**7, transcendentals=0),
@@ -233,16 +252,34 @@
     ln = lax.broadcasted_iota(jnp.int32, VREG, 1)
     sb = lax.broadcasted_iota(jnp.int32, VREG, 0)
     el = lambda c, j: rows_of(c[j // 8], j % 8)
-    c0 = {0: lane_of(W[t][0], o)}
-    c1 = {0: lane_of(W[t][0], o + 1)}
+    c0 = [lane_of(W[t][v], o) for v in range(nv)]
+    c1 = [lane_of(W[t][v], o + 1) for v in range(nv)]
     D = inv2(el(c0, 0), el(c1, 0), el(c0, 1), el(c1, 1))
     for j in range(0, 8 * nv, 2):
         l = o + j
-        c0 = [lane_of(W[t][v], l) for v in range(nv)]
-        c1 = [lane_of(W[t][v], l + 1) for v in range(nv)]
         i00, n01, n10, i11 = D
         ar = ln == l
         ab = ar | (ln == l + 1)
+
+        def rows_in(v, X, s0, s1):
+            if j // 8 != v:
+                return X
+            return tuple(jnp.where(sb == j % 8, s0[k], jnp.where(sb == j % 8 + 1, s1[k], X[k])) for k in range(2))
+
+        last = j + 2 == 8 * nv
+        if not last:
+            nxt, pivot = [], []
+            for ahead in (l + 2, l + 3):
+                d = [lane_of(W[t][v], ahead) for v in range(nv)]
+                a, c = el(d, j), el(d, j + 1)
+                s0 = csub(cmul(i00, a), cmul(n01, c))
+                s1 = csub(cmul(i11, c), cmul(n10, a))
+                for k in (j + 2, j + 3):
+                    pivot.append(csub(el(d, k), cadd(cmul(el(c0, k), s0), cmul(el(c1, k), s1))))
+                nxt.append(
+                    [rows_in(v, csub(d[v], cadd(cmul(c0[v], s0), cmul(c1[v], s1))), s0, s1) for v in range(nv)]
+                )
+            D = inv2(pivot[0], pivot[2], pivot[1], pivot[3])
         new = []
         for s in range(2):
             r0 = rows_of(W[s][j // 8], j % 8)
@@ -257,25 +294,11 @@
                 X = W[s][v]
                 if s == t:
                     X = (jnp.where(ab, 0.0, X[0]), jnp.where(ab, 0.0, X[1]))
-                X = csub(X, cadd(cmul(c0[v], s0), cmul(c1[v], s1)))
-                if j // 8 == v:
-                    X = tuple(
-                        jnp.where(sb == j % 8, s0[k], jnp.where(sb == j % 8 + 1, s1[k], X[k])) for k in range(2)
-                    )
-                col.append(X)
+                col.append(rows_in(v, csub(X, cadd(cmul(c0[v], s0), cmul(c1[v], s1))), s0, s1))
             new.append(col)
-        if j + 2 < 8 * nv:
-            vs = sorted({j // 8, (j + 2) // 8})
-            pivot = []
-            for ahead in (l + 2, l + 3):
-                d = {v: lane_of(W[t][v], ahead) for v in vs}
-                a, c = el(d, j), el(d, j + 1)
-                s0 = csub(cmul(i00, a), cmul(n01, c))
-                s1 = csub(cmul(i11, c), cmul(n10, a))
-                for k in (j + 2, j + 3):
-                    pivot.append(csub(el(d, k), cadd(cmul(el(c0, k), s0), cmul(el(c1, k), s1))))
-            D = inv2(pivot[0], pivot[2], pivot[1], pivot[3])
         W = new
+        if not last:
+            c0, c1 = nxt
     return W
 
 
@@ -386,15 +409,38 @@
     re[...], im[...] = x
 
 
-def green_kernel(place_ref, level_ref, all_ref, out_ref, outer, work, near, side_term, lefts, scr):
+def green_kernel(
+    energy_ref, broadening_ref, contact_ref, offset_ref, weight_ref, herm_ref, hop_ref, out_ref, reach_ref,
+    outer, work, near, side_term, lefts, scr,
+):
     rows_of = Rows(scr)
-    place = place_ref[0]
+    place = lax.axis_index("space")
+    point, points = lax.axis_index("energy"), lax.axis_size("energy")
     side = place // 2
-    e, eta, c = level_ref[0], level_ref[1], level_ref[2]
-    eye = (lax.broadcasted_iota(jnp.int32, (N, N), 0) == lax.broadcasted_iota(jnp.int32, (N, N), 1)).astype(f32)
-    herm = lambda k: (all_ref[k, 0], all_ref[k, 1])
-    hop = lambda k: (all_ref[k, 2], all_ref[k, 3])
-    back = lambda k: (all_ref[k, 2].T, -all_ref[k, 3].T)
+    e, eta, c = energy_ref[0], broadening_ref[0], contact_ref[0]
+
+    even = lax.rem(point, 2) == 0
+    reach = [-2, 2, -4, 4] + [jnp.where(even, a, b) for a, b in ((1, -1), (-1, -3), (3, 1), (-3, 3))]
+    for k, d in enumerate(reach):
+        inside = (point + d >= 0) & (point + d < points)
+        total = jnp.float32(0.0)
+        for j in range(8):
+            total = total + jnp.where(inside & (offset_ref[0, j] == d), weight_ref[0, j], 0.0)
+        reach_ref[k] = total
+
+    row, column = triangles()
+    eye = (row == column).astype(f32)
+
+    def herm(k):
+        mixed = herm_ref[k]
+        turned = mixed.T
+        return (
+            jnp.where(row <= column, mixed, turned),
+            jnp.where(row > column, mixed, jnp.where(row < column, -turned, 0.0)),
+        )
+
+    hop = lambda k: (hop_ref[k, 0], hop_ref[k, 1])
+    back = lambda k: (hop_ref[k, 0].T, -hop_ref[k, 1].T)
 
     gram = product(hop(0), back(0))
     h0, h3 = herm(0), herm(3)
@@ -451,15 +497,15 @@
         put(out_ref, cadd(own, product(pair(side_term), product(pair(work), left))))
 
 
-def green_block(place, levels, everything):
+def green_block(energy, broadening, contact, offset, weight, herms, hops):
     vmem = pl.BlockSpec(memory_space=pltpu.VMEM)
     smem = pl.BlockSpec(memory_space=pltpu.SMEM)
     block = pltpu.VMEM((2, N, N), f32)
     return pl.pallas_call(
         green_kernel,
-        out_shape=jax.ShapeDtypeStruct((2, N, N), f32),
-        in_specs=[smem, smem, vmem],
-        out_specs=vmem,
+        out_shape=(jax.ShapeDtypeStruct((2, N, N), f32), jax.ShapeDtypeStruct((8,), f32)),
+        in_specs=[smem] * 5 + [vmem] * 2,
+        out_specs=(vmem, smem),
         scratch_shapes=[
             pltpu.VMEM((2, 2, N, N), f32),
             block,
@@ -470,21 +516,13 @@
         ],
         compiler_params=pltpu.CompilerParams(vmem_limit_bytes=48 << 20),
         cost_estimate=pl.CostEstimate(flops=10**10, bytes_accessed=10**7, transcendentals=0),
-    )(place, levels, everything)
+    )(energy, broadening, contact, offset, weight, herms, hops)
 
 
 def per_device(ham_blocks, hopping, energy, broadening, contact, phonon_offset, phonon_weight):
-    place = lax.axis_index("space").astype(jnp.int32).reshape(1)
-    point = lax.axis_index("energy").astype(jnp.int32)
-    points = lax.axis_size("energy")
-    everything = gathered(ham_blocks[0], hopping[0])
-    green = green_block(place, jnp.concatenate([energy, broadening, contact]), everything)
-    offsets, weights = phonon_offset[0], phonon_weight[0]
-    inside = (point + offsets >= 0) & (point + offsets < points)
-    even = point % 2 == 0
-    reach = [-2, 2, -4, 4] + [jnp.where(even, a, b) for a, b in ((1, -1), (-1, -3), (3, 1), (-3, 3))]
-    weight_of = jnp.stack([jnp.sum(jnp.where(inside & (offsets == d), weights, 0.0)) for d in reach])
-    total = phonon_sum(weight_of, green.reshape(512, N)).reshape(2, N, N)
+    herms, hops = gathered(ham_blocks[0], hopping[0])
+    green, reach = green_block(energy, broadening, contact, phonon_offset, phonon_weight, herms, hops)
+    total = phonon_sum(reach, green.reshape(512, N)).reshape(2, N, N)
     return (green[None, None], total[None, None])
 
 

time: 126 us -> 122 us (0.968)
  local copies, waits for them, and re-layouts: 8.94 us -> 5.21 us
  other arithmetic: 1.45 us -> 0 us
    another operation x1 -> x0, local copies, waits for them, and re-layouts: 5.02 us -> none  [per_device(): jnp.stack([jnp.sum(jnp.where(inside & (offsets == d), weights, 0.0)) for...]
    reduce_sum x1 -> x0, other arithmetic: 1.37 us -> none  [per_device(): jnp.sum(jnp.where(inside & (offsets == d), weights, 0.0))]
    unnamed x7 -> x11, local copies, waits for them, and re-layouts: 3.92 us -> 5.21 us
where the time goes in v3:
time: 122 us; the launch traced here: 121 us
  Pallas kernels  114 us (93%)
  local copies, waits for them, and re-layouts  5.21 us (4%)
  between operations  2.62 us (2%)
    pallas_call x1, Pallas kernels, green_block(): pl.pallas_call(green_kernel, out_shape=(jax.ShapeDtypeStruct((2, N, N), f...  58.3 us
    pallas_call x1, Pallas kernels, phonon_sum(): pl.pallas_call(phonon_kernel, out_shape=jax.ShapeDtypeStruct(block, f32),...  35.2 us
    pallas_call x1, Pallas kernels, gathered(): pl.pallas_call(gather_kernel, out_shape=(jax.ShapeDtypeStruct((4, N, N),...  20.1 us
    unnamed x11, local copies, waits for them, and re-layouts  5.21 us

profile of v3, /device:TPU:1, one launch (start us, length us, event | category | flops | bytes accessed | tf_op | source)
XLA Modules:
  0.0 121.4 jit_solution(970834457140862058)
XLA Ops:
  2.6 0.0 copy-start
  2.6 1.0 copy-done
  3.6 0.0 copy-start.1
  3.6 1.0 copy-done.1
  4.7 20.1 %shard_map.86 = (f32[4,256,256]{2,1,0:T(8,128)S(1)}, f32[4,2,256,256]{3,2,1,0:T(8,128)S(1)}) custom-call(f32[2,256,256]{2,1,0:T(8,128)S(1)} %bitcast.6, f32[2,256,256]{2,1,0:T(8,128)S(1)} %bitcast.7), custom_call_target="tpu_custom_call" | custom-call | flops 1000000 | bytes 10000000 | tf_op jit(solution)/shard_map/pallas_call | solution.py:113
  24.8 0.0 copy-start.3
  24.8 0.6 copy-done.3
  25.4 0.0 copy-start.4
  25.4 0.7 copy-done.4
  26.1 58.3 %shard_map.87 = (f32[2,256,256]{2,1,0:T(8,128)}, f32[8]{0:T(128)S(1)}) custom-call(f32[1]{0:T(128)S(6)} %copy.10.energy_ref, f32[1]{0:T(128)S(6)} %copy.11.broadening_ref, f32[1]{0:T(128)S(6)} %copy.12.contact_ref, s32[1,8]{1,0:T(1,128)S(1)} %copy-done.3, f32[1,8]{1,0:T(1,128)S(1)} %copy-done.4, f32[4,256,256]{2,1,0:T(8,128)S(1)} %get-tuple-element.6.herm_ref, ...), custom_call_target="tpu_custom_call" | custom-call | flops 10000000000 | bytes 10000000 | tf_op jit(solution)/shard_map/pallas_call | solution.py:504
  84.4 0.0 copy-start.2
  84.4 1.0 copy-done.2
  85.4 35.2 %shard_map.88 = f32[512,256]{1,0:T(8,128)S(1)} custom-call(f32[8]{0:T(128)S(1)} %get-tuple-element.9.weight_ref, f32[512,256]{1,0:T(8,128)S(1)} %bitcast.9), custom_call_target="tpu_custom_call" | custom-call | flops 1000000 | bytes 10000000 | tf_op jit(solution)/shard_map/pallas_call | solution.py:193
  120.6 0.8 copy.13
Async XLA Ops:
  2.6 1.0 copy-start
  3.6 1.0 copy-start.1
  24.8 0.7 copy-start.3
  25.4 0.7 copy-start.4
  84.4 1.0 copy-start.2

commit v4 on v3

--- a/solution.py
+++ b/solution.py
@@ -113,7 +113,7 @@
     return pl.pallas_call(
         gather_kernel,
         out_shape=(jax.ShapeDtypeStruct((4, N, N), f32), jax.ShapeDtypeStruct((4, 2, N, N), f32)),
-        in_specs=[anywhere, anywhere],
+        in_specs=[pl.BlockSpec(memory_space=pltpu.HBM)] * 2,
         out_specs=(anywhere, anywhere),
         scratch_shapes=[
             pltpu.VMEM((2, N, N), f32),
@@ -193,7 +193,7 @@
     return pl.pallas_call(
         phonon_kernel,
         out_shape=jax.ShapeDtypeStruct(block, f32),
-        in_specs=[pl.BlockSpec(memory_space=pltpu.SMEM), vmem],
+        in_specs=[pl.BlockSpec(memory_space=pltpu.SMEM), pl.BlockSpec(memory_space=pltpu.HBM)],
         out_specs=vmem,
         scratch_shapes=[
             pltpu.VMEM((2, *block), f32),
@@ -302,6 +302,57 @@
     return W
 
 
+def eliminate_rows_of_two(W, t, o, rows_of):
+    nv = len(W[0])
+    ln = lax.broadcasted_iota(jnp.int32, VREG, 1)
+    sb = lax.broadcasted_iota(jnp.int32, VREG, 0)
+    el = lambda c, j: rows_of(c[j // 8], j % 8)
+    c0 = {0: lane_of(W[t][0], o)}
+    c1 = {0: lane_of(W[t][0], o + 1)}
+    D = inv2(el(c0, 0), el(c1, 0), el(c0, 1), el(c1, 1))
+    for j in range(0, 8 * nv, 2):
+        l = o + j
+        c0 = [lane_of(W[t][v], l) for v in range(nv)]
+        c1 = [lane_of(W[t][v], l + 1) for v in range(nv)]
+        i00, n01, n10, i11 = D
+        ar = ln == l
+        ab = ar | (ln == l + 1)
+        new = []
+        for s in range(2):
+            r0 = rows_of(W[s][j // 8], j % 8)
+            r1 = rows_of(W[s][(j + 1) // 8], (j + 1) % 8)
+            if s == t:
+                r0 = (jnp.where(ab, jnp.where(ar, 1.0, 0.0), r0[0]), jnp.where(ab, 0.0, r0[1]))
+                r1 = (jnp.where(ab, jnp.where(ar, 0.0, 1.0), r1[0]), jnp.where(ab, 0.0, r1[1]))
+            s0 = csub(cmul(i00, r0), cmul(n01, r1))
+            s1 = csub(cmul(i11, r1), cmul(n10, r0))
+            col = []
+            for v in range(nv):
+                X = W[s][v]
+                if s == t:
+                    X = (jnp.where(ab, 0.0, X[0]), jnp.where(ab, 0.0, X[1]))
+                X = csub(X, cadd(cmul(c0[v], s0), cmul(c1[v], s1)))
+                if j // 8 == v:
+                    X = tuple(
+                        jnp.where(sb == j % 8, s0[k], jnp.where(sb == j % 8 + 1, s1[k], X[k])) for k in range(2)
+                    )
+                col.append(X)
+            new.append(col)
+        if j + 2 < 8 * nv:
+            vs = sorted({j // 8, (j + 2) // 8})
+            pivot = []
+            for ahead in (l + 2, l + 3):
+                d = {v: lane_of(W[t][v], ahead) for v in vs}
+                a, c = el(d, j), el(d, j + 1)
+                s0 = csub(cmul(i00, a), cmul(n01, c))
+                s1 = csub(cmul(i11, c), cmul(n10, a))
+                for k in (j + 2, j + 3):
+                    pivot.append(csub(el(d, k), cadd(cmul(el(c0, k), s0), cmul(el(c1, k), s1))))
+            D = inv2(pivot[0], pivot[2], pivot[1], pivot[3])
+        W = new
+    return W
+
+
 def halves(x):
     high = x.astype(bf16)
     return high, (x - high.astype(f32)).astype(bf16)
@@ -338,10 +389,13 @@
     return stacked(around(first) + around(second), 0)
 
 
-def invert(mats, rows_of):
+def invert(mats, rows_of, beside=None):
     def tile_steps(tile, carry):
         columns = [pl.ds(pl.multiple_of(128 * tile, 128), 128), pl.ds(pl.multiple_of(128 - 128 * tile, 128), 128)]
         rows_of.kept.clear()
+        if beside is not None:
+            beside(tile)
+        eliminate = eliminate_rows if len(mats) == 1 else eliminate_rows_of_two
 
         def rows(q, height):
             return pl.ds(pl.multiple_of(128 * tile + SUB * q, SUB), height)
@@ -356,7 +410,7 @@
             here = (ln >= o) & (ln < o + SUB)
             lefts = [left_panel([M[k][:, columns[0]] for k in range(2)], o) for M in mats]
             strips = [left_panel([M[k][rows((q + 1) % 4, SUB), columns[0]] for k in range(2)], o) for M in mats]
-            panels = [eliminate_rows(W, 0, o, rows_of) for W in panels]
+            panels = [eliminate(W, 0, o, rows_of) for W in panels]
             following = []
             for M, L, W in zip(mats, lefts, panels):
                 R = right_panel(W, o)
@@ -411,7 +465,7 @@
 
 def green_kernel(
     energy_ref, broadening_ref, contact_ref, offset_ref, weight_ref, herm_ref, hop_ref, out_ref, reach_ref,
-    outer, work, near, side_term, lefts, scr,
+    bank, work, scr,
 ):
     rows_of = Rows(scr)
     place = lax.axis_index("space")
@@ -444,43 +498,48 @@
 
     gram = product(hop(0), back(0))
     h0, h3 = herm(0), herm(3)
-    put(planes(outer.at[0]), (e * eye - h0[0] - c * gram[1], eta * eye - h0[1] + c * gram[0]))
-    put(planes(outer.at[1]), (e * eye - h3[0], (eta + c) * eye - h3[1]))
-    put(planes(lefts.at[0]), back(1))
-    put(planes(lefts.at[1]), hop(1))
-    put(planes(lefts.at[2]), hop(3))
-    put(planes(lefts.at[3]), back(3))
+    put(planes(bank.at[0]), (e * eye - h0[0] - c * gram[1], eta * eye - h0[1] + c * gram[0]))
+    put(planes(bank.at[1]), (e * eye - h3[0], (eta + c) * eye - h3[1]))
+    put(planes(bank.at[2]), back(1))
+    put(planes(bank.at[3]), hop(1))
+    put(planes(bank.at[4]), hop(3))
+    put(planes(bank.at[5]), back(3))
 
     @pl.when(side == 0)
     def _():
-        put(planes(lefts.at[4]), hop(2))
-        put(planes(lefts.at[5]), back(2))
+        put(planes(bank.at[6]), hop(2))
+        put(planes(bank.at[7]), back(2))
 
     @pl.when(side == 1)
     def _():
-        put(planes(lefts.at[4]), back(2))
-        put(planes(lefts.at[5]), hop(2))
-
-    invert([planes(outer.at[0]), planes(outer.at[1])], rows_of)
+        put(planes(bank.at[6]), back(2))
+        put(planes(bank.at[7]), hop(2))
+
+    invert([planes(bank.at[0]), planes(bank.at[1])], rows_of)
 
     def inner(i, sigma):
         h = herm(i)
         return (e * eye - h[0] - sigma[0], eta * eye - h[1] - sigma[1])
 
     far = 1 - side
-    right = product(pair(outer.at[far]), pair(lefts.at[2 * far + 1]))
-    put(work, inner(1 + far, product(pair(lefts.at[2 * far]), right)))
-    right = product(pair(outer.at[side]), pair(lefts.at[2 * side + 1]))
-    put(side_term, right)
-    put(near, inner(1 + side, product(pair(lefts.at[2 * side]), right)))
+    near_l, near_r = 2 + 2 * side, 3 + 2 * side
+    right = product(pair(bank.at[far]), pair(bank.at[2 * far + 3]))
+    put(work, inner(1 + far, product(pair(bank.at[2 * far + 2]), right)))
 
     def solve(step, carry):
-        invert([planes(work)], rows_of)
+        def near_product(tile):
+            job = 2 * step + tile
+            first = jnp.where(job == 0, side, near_l)
+            second = jnp.where(job == 0, near_r, jnp.where(job == 1, 8, side))
+            put(bank.at[jnp.where(job == 0, 8, jnp.where(job == 1, 9, 10))], product(pair(bank.at[first]), pair(bank.at[second])))
+
+        invert([planes(work)], rows_of, near_product)
 
         @pl.when(step == 0)
         def _():
-            right = product(pair(work), pair(lefts.at[5]))
-            put(work, csub(pair(near), product(pair(lefts.at[4]), right)))
+            right = product(pair(work), pair(bank.at[7]))
+            middle = product(pair(bank.at[6]), right)
+            put(work, inner(1 + side, cadd(pair(bank.at[9]), middle)))
 
         return carry
 
@@ -492,9 +551,7 @@
 
     @pl.when((place == 0) | (place == 3))
     def _():
-        own = pair(outer.at[side])
-        left = product(pair(lefts.at[2 * side]), own)
-        put(out_ref, cadd(own, product(pair(side_term), product(pair(work), left))))
+        put(out_ref, cadd(pair(bank.at[side]), product(pair(bank.at[8]), product(pair(work), pair(bank.at[10])))))
 
 
 def green_block(energy, broadening, contact, offset, weight, herms, hops):
@@ -507,11 +564,8 @@
         in_specs=[smem] * 5 + [vmem] * 2,
         out_specs=(vmem, smem),
         scratch_shapes=[
-            pltpu.VMEM((2, 2, N, N), f32),
+            pltpu.VMEM((11, 2, N, N), f32),
             block,
-            block,
-            block,
-            pltpu.VMEM((6, 2, N, N), f32),
             pltpu.VMEM((8 * SLOTS, 128), f32),
         ],
         compiler_params=pltpu.CompilerParams(vmem_limit_bytes=48 << 20),

time: 122 us -> 118 us (0.967)
  Pallas kernels: 114 us -> 110 us
    pallas_call x1, Pallas kernels: 58.3 us -> 54.3 us  [green_block(): pl.pallas_call(green_kernel, out_shape=(jax.ShapeDtypeStruct((2, N, N), f...]
where the time goes in v4:
time: 118 us; the launch traced here: 117 us
  Pallas kernels  110 us (93%)
  local copies, waits for them, and re-layouts  5.21 us (4%)
  between operations  2.62 us (2%)
    pallas_call x1, Pallas kernels, green_block(): pl.pallas_call(green_kernel, out_shape=(jax.ShapeDtypeStruct((2, N, N), f...  54.3 us
    pallas_call x1, Pallas kernels, phonon_sum(): pl.pallas_call(phonon_kernel, out_shape=jax.ShapeDtypeStruct(block, f32),...  35.2 us
    pallas_call x1, Pallas kernels, gathered(): pl.pallas_call(gather_kernel, out_shape=(jax.ShapeDtypeStruct((4, N, N),...  20.1 us
    unnamed x11, local copies, waits for them, and re-layouts  5.21 us

profile of v4, /device:TPU:1, one launch (start us, length us, event | category | flops | bytes accessed | tf_op | source)
XLA Modules:
  0.0 117.4 jit_solution(14265834357135760054)
XLA Ops:
  2.6 0.0 copy-start
  2.6 1.0 copy-done
  3.6 0.0 copy-start.1
  3.6 1.0 copy-done.1
  4.7 20.1 %shard_map.86 = (f32[4,256,256]{2,1,0:T(8,128)S(1)}, f32[4,2,256,256]{3,2,1,0:T(8,128)S(1)}) custom-call(f32[2,256,256]{2,1,0:T(8,128)S(1)} %bitcast.6, f32[2,256,256]{2,1,0:T(8,128)S(1)} %bitcast.7), custom_call_target="tpu_custom_call" | custom-call | flops 1000000 | bytes 10000000 | tf_op jit(solution)/shard_map/pallas_call | solution.py:113
  24.8 0.0 copy-start.3
  24.8 0.6 copy-done.3
  25.4 0.0 copy-start.4
  25.4 0.7 copy-done.4
  26.1 54.3 %shard_map.87 = (f32[2,256,256]{2,1,0:T(8,128)}, f32[8]{0:T(128)S(1)}) custom-call(f32[1]{0:T(128)S(6)} %copy.10.energy_ref, f32[1]{0:T(128)S(6)} %copy.11.broadening_ref, f32[1]{0:T(128)S(6)} %copy.12.contact_ref, s32[1,8]{1,0:T(1,128)S(1)} %copy-done.3, f32[1,8]{1,0:T(1,128)S(1)} %copy-done.4, f32[4,256,256]{2,1,0:T(8,128)S(1)} %get-tuple-element.6.herm_ref, ...), custom_call_target="tpu_custom_call" | custom-call | flops 10000000000 | bytes 10000000 | tf_op jit(solution)/shard_map/pallas_call | solution.py:561
  80.4 0.0 copy-start.2
  80.4 1.0 copy-done.2
  81.5 35.2 %shard_map.88 = f32[512,256]{1,0:T(8,128)S(1)} custom-call(f32[8]{0:T(128)S(1)} %get-tuple-element.9.weight_ref, f32[512,256]{1,0:T(8,128)S(1)} %bitcast.9), custom_call_target="tpu_custom_call" | custom-call | flops 1000000 | bytes 10000000 | tf_op jit(solution)/shard_map/pallas_call | solution.py:193
  116.6 0.8 copy.13
Async XLA Ops:
  2.6 1.0 copy-start
  3.6 1.0 copy-start.1
  24.8 0.7 copy-start.3
  25.4 0.7 copy-start.4
  80.4 1.0 copy-start.2

commit v5 on v4

--- a/solution.py
+++ b/solution.py
@@ -134,7 +134,6 @@
     after, before = {"energy": lax.rem(point + 2, points)}, {"energy": lax.rem(point + points - 2, points)}
     beside = {"energy": point + 1 - 2 * core}
     along = (after, before)
-    greet((after, before, beside))
     started = []
 
     def piece(i):
@@ -159,23 +158,53 @@
             total = total + weight_ref[k] * ref[piece(i)]
         out_ref[piece(i)] = total
 
+    chip, chips = point // 2, points // 2
+    sends = (chip < chips - 1, chip > 0)
+    gets = (chip > 0, chip < chips - 1)
+    relays = (sends[0] & gets[0], sends[1] & gets[1])
+    gets_far = (chip > 1, chip < chips - 2)
+    for d in range(2):
+        for ref, reached in ((near, gets[d]), (far, gets_far[d])):
+
+            @pl.when(jnp.logical_not(reached))
+            def _():
+                ref[d] = jnp.zeros_like(ref[d])
+
+    greet((after, before, beside))
     first, second, swap = {}, {}, {}
+    waits = []
+
+    def send_if(condition, source, target, to, slot):
+        copy = pltpu.make_async_remote_copy(
+            src_ref=source,
+            dst_ref=target,
+            send_sem=send_sem.at[slot],
+            recv_sem=recv_sem.at[slot],
+            device_id=to,
+            device_id_type=MESH,
+        )
+        pl.when(condition)(copy.start)
+        waits.append((condition, copy))
+        return copy
+
     for i in range(CHUNKS):
         for d in range(2):
-            first[d, i] = send(green_ref.at[piece(i)], near.at[d, piece(i)], along[d], d * CHUNKS + i)
+            first[d, i] = send_if(sends[d], green_ref.at[piece(i)], near.at[d, piece(i)], along[d], d * CHUNKS + i)
     for i in range(CHUNKS):
         swap[0, i] = send(green_ref.at[piece(i)], side.at[0, piece(i)], beside, 4 * CHUNKS + i)
     for i in range(CHUNKS):
         for d in range(2):
-            first[d, i].wait_recv()
-            second[d, i] = send(near.at[d, piece(i)], far.at[d, piece(i)], along[d], (2 + d) * CHUNKS + i)
+            pl.when(gets[d])(first[d, i].wait_recv)
+            second[d, i] = send_if(
+                relays[d], near.at[d, piece(i)], far.at[d, piece(i)], along[d], (2 + d) * CHUNKS + i
+            )
             swap[1 + d, i] = send(near.at[d, piece(i)], side.at[1 + d, piece(i)], beside, (5 + d) * CHUNKS + i)
         swap[0, i].wait_recv()
         out_ref[piece(i)] = weight_ref[4] * side[0, piece(i)]
         add(i, [(0, near.at[0]), (1, near.at[1])])
     for i in range(CHUNKS):
-        second[0, i].wait_recv()
-        second[1, i].wait_recv()
+        for d in range(2):
+            pl.when(gets_far[d])(second[d, i].wait_recv)
         swap[3, i] = send(far.at[1 - core, piece(i)], side.at[3, piece(i)], beside, 7 * CHUNKS + i)
         swap[1, i].wait_recv()
         swap[2, i].wait_recv()
@@ -185,6 +214,8 @@
         add(i, [(7, side.at[3])])
     for copy in started:
         copy.wait_send()
+    for condition, copy in waits:
+        pl.when(condition)(copy.wait_send)
 
 
 def phonon_sum(weights, green):
@@ -193,7 +224,7 @@
     return pl.pallas_call(
         phonon_kernel,
         out_shape=jax.ShapeDtypeStruct(block, f32),
-        in_specs=[pl.BlockSpec(memory_space=pltpu.SMEM), pl.BlockSpec(memory_space=pltpu.HBM)],
+        in_specs=[pl.BlockSpec(memory_space=pltpu.SMEM), pl.BlockSpec(memory_space=pl.ANY)],
         out_specs=vmem,
         scratch_shapes=[
             pltpu.VMEM((2, *block), f32),
@@ -464,7 +495,7 @@
 
 
 def green_kernel(
-    energy_ref, broadening_ref, contact_ref, offset_ref, weight_ref, herm_ref, hop_ref, out_ref, reach_ref,
+    energy_ref, broadening_ref, contact_ref, offset_ref, weight_ref, herm_ref, hop_ref, out_ref, reach_ref, kept_ref,
     bank, work, scr,
 ):
     rows_of = Rows(scr)
@@ -545,13 +576,17 @@
 
     lax.fori_loop(0, 2, solve, 0)
 
+    def finish(x):
+        put(out_ref, x)
+        put(kept_ref, x)
+
     @pl.when((place == 1) | (place == 2))
     def _():
-        put(out_ref, pair(work))
+        finish(pair(work))
 
     @pl.when((place == 0) | (place == 3))
     def _():
-        put(out_ref, cadd(pair(bank.at[side]), product(pair(bank.at[8]), product(pair(work), pair(bank.at[10])))))
+        finish(cadd(pair(bank.at[side]), product(pair(bank.at[8]), product(pair(work), pair(bank.at[10])))))
 
 
 def green_block(energy, broadening, contact, offset, weight, herms, hops):
@@ -560,9 +595,13 @@
     block = pltpu.VMEM((2, N, N), f32)
     return pl.pallas_call(
         green_kernel,
-        out_shape=(jax.ShapeDtypeStruct((2, N, N), f32), jax.ShapeDtypeStruct((8,), f32)),
+        out_shape=(
+            jax.ShapeDtypeStruct((2, N, N), f32),
+            jax.ShapeDtypeStruct((8,), f32),
+            jax.ShapeDtypeStruct((2, N, N), f32),
+        ),
         in_specs=[smem] * 5 + [vmem] * 2,
-        out_specs=(vmem, smem),
+        out_specs=(vmem, smem, vmem),
         scratch_shapes=[
             pltpu.VMEM((11, 2, N, N), f32),
             block,
@@ -575,8 +614,8 @@
 
 def per_device(ham_blocks, hopping, energy, broadening, contact, phonon_offset, phonon_weight):
     herms, hops = gathered(ham_blocks[0], hopping[0])
-    green, reach = green_block(energy, broadening, contact, phonon_offset, phonon_weight, herms, hops)
-    total = phonon_sum(reach, green.reshape(512, N)).reshape(2, N, N)
+    green, reach, kept = green_block(energy, broadening, contact, phonon_offset, phonon_weight, herms, hops)
+    total = phonon_sum(reach, kept.reshape(512, N)).reshape(2, N, N)
     return (green[None, None], total[None, None])
 
 

time: 118 us -> 114 us (0.966)
  the two profiles are of different devices: /device:TPU:1 before, /device:TPU:7 now
where the time goes in v5:
time: 114 us
  Pallas kernels  107 us (94%)
  local copies, waits for them, and re-layouts  4.18 us (4%)
  between operations  2.61 us (2%)
    pallas_call x1, Pallas kernels, green_block(): pl.pallas_call(green_kernel, out_shape=(jax.ShapeDtypeStruct((2, N, N), f...  54.3 us
    pallas_call x1, Pallas kernels, phonon_sum(): pl.pallas_call(phonon_kernel, out_shape=jax.ShapeDtypeStruct(block, f32),...  33.4 us
    pallas_call x1, Pallas kernels, gathered(): pl.pallas_call(gather_kernel, out_shape=(jax.ShapeDtypeStruct((4, N, N),...  19.3 us
    unnamed x9, local copies, waits for them, and re-layouts  4.18 us

profile of v5, /device:TPU:7, one launch (start us, length us, event | category | flops | bytes accessed | tf_op | source)
XLA Modules:
  0.0 113.8 jit_solution(9001451426679194372)
XLA Ops:
  2.6 0.0 copy-start
  2.6 1.0 copy-done
  3.6 0.0 copy-start.1
  3.6 1.0 copy-done.1
  4.7 19.3 %shard_map.86 = (f32[4,256,256]{2,1,0:T(8,128)S(1)}, f32[4,2,256,256]{3,2,1,0:T(8,128)S(1)}) custom-call(f32[2,256,256]{2,1,0:T(8,128)S(1)} %bitcast.6, f32[2,256,256]{2,1,0:T(8,128)S(1)} %bitcast.7), custom_call_target="tpu_custom_call" | custom-call | flops 1000000 | bytes 10000000 | tf_op jit(solution)/shard_map/pallas_call | solution.py:113
  23.9 0.0 copy-start.2
  23.9 0.6 copy-done.2
  24.6 0.0 copy-start.3
  24.6 0.7 copy-done.3
  25.2 54.3 %shard_map.87 = (f32[2,256,256]{2,1,0:T(8,128)}, f32[8]{0:T(128)S(1)}, f32[2,256,256]{2,1,0:T(8,128)S(1)}) custom-call(f32[1]{0:T(128)S(6)} %copy.10.energy_ref, f32[1]{0:T(128)S(6)} %copy.11.broadening_ref, f32[1]{0:T(128)S(6)} %copy.12.contact_ref, s32[1,8]{1,0:T(1,128)S(1)} %copy-done.2, f32[1,8]{1,0:T(1,128)S(1)} %copy-done.3, ...), custom_call_target="tpu_custom_call" | custom-call | flops 10000000000 | bytes 10000000 | tf_op jit(solution)/shard_map/pallas_call | solution.py:596
  79.6 33.4 %shard_map.88 = f32[512,256]{1,0:T(8,128)S(1)} custom-call(f32[8]{0:T(128)S(1)} %get-tuple-element.10.weight_ref, f32[512,256]{1,0:T(8,128)S(1)} %bitcast.8), custom_call_target="tpu_custom_call" | custom-call | flops 1000000 | bytes 10000000 | tf_op jit(solution)/shard_map/pallas_call | solution.py:224
  113.0 0.8 copy.13
Async XLA Ops:
  2.6 1.0 copy-start
  3.6 1.0 copy-start.1
  23.9 0.7 copy-start.2
  24.6 0.7 copy-start.3

commit v6 on v5

--- a/solution.py
+++ b/solution.py
@@ -15,7 +15,7 @@
 SLOTS = 256
 
 
-CHUNKS = 8
+CHUNKS = 4
 PIECE = 512 // CHUNKS
 MESH = pl.DeviceIdType.MESH
 

time: 114 us -> 113 us (level)
  no operation moved by 1% of the time
where the time goes in v6:
time: 113 us
  Pallas kernels  106 us (94%)
  local copies, waits for them, and re-layouts  4.18 us (4%)
  between operations  2.61 us (2%)
    pallas_call x1, Pallas kernels, green_block(): pl.pallas_call(green_kernel, out_shape=(jax.ShapeDtypeStruct((2, N, N), f...  54.3 us
    pallas_call x1, Pallas kernels, phonon_sum(): pl.pallas_call(phonon_kernel, out_shape=jax.ShapeDtypeStruct(block, f32),...  32.9 us
    pallas_call x1, Pallas kernels, gathered(): pl.pallas_call(gather_kernel, out_shape=(jax.ShapeDtypeStruct((4, N, N),...  19.3 us
    unnamed x9, local copies, waits for them, and re-layouts  4.18 us

profile of v6, /device:TPU:7, one launch (start us, length us, event | category | flops | bytes accessed | tf_op | source)
XLA Modules:
  0.0 113.3 jit_solution(17944693871905346400)
XLA Ops:
  2.6 0.0 copy-start
  2.6 1.0 copy-done
  3.6 0.0 copy-start.1
  3.6 1.0 copy-done.1
  4.7 19.3 %shard_map.86 = (f32[4,256,256]{2,1,0:T(8,128)S(1)}, f32[4,2,256,256]{3,2,1,0:T(8,128)S(1)}) custom-call(f32[2,256,256]{2,1,0:T(8,128)S(1)} %bitcast.6, f32[2,256,256]{2,1,0:T(8,128)S(1)} %bitcast.7), custom_call_target="tpu_custom_call" | custom-call | flops 1000000 | bytes 10000000 | tf_op jit(solution)/shard_map/pallas_call | solution.py:113
  23.9 0.0 copy-start.2
  23.9 0.6 copy-done.2
  24.6 0.0 copy-start.3
  24.6 0.7 copy-done.3
  25.2 54.3 %shard_map.87 = (f32[2,256,256]{2,1,0:T(8,128)}, f32[8]{0:T(128)S(1)}, f32[2,256,256]{2,1,0:T(8,128)S(1)}) custom-call(f32[1]{0:T(128)S(6)} %copy.10.energy_ref, f32[1]{0:T(128)S(6)} %copy.11.broadening_ref, f32[1]{0:T(128)S(6)} %copy.12.contact_ref, s32[1,8]{1,0:T(1,128)S(1)} %copy-done.2, f32[1,8]{1,0:T(1,128)S(1)} %copy-done.3, ...), custom_call_target="tpu_custom_call" | custom-call | flops 10000000000 | bytes 10000000 | tf_op jit(solution)/shard_map/pallas_call | solution.py:596
  79.6 32.9 %shard_map.88 = f32[512,256]{1,0:T(8,128)S(1)} custom-call(f32[8]{0:T(128)S(1)} %get-tuple-element.10.weight_ref, f32[512,256]{1,0:T(8,128)S(1)} %bitcast.8), custom_call_target="tpu_custom_call" | custom-call | flops 1000000 | bytes 10000000 | tf_op jit(solution)/shard_map/pallas_call | solution.py:224
  112.5 0.8 copy.13
Async XLA Ops:
  2.6 1.0 copy-start
  3.6 1.0 copy-start.1
  23.9 0.7 copy-start.2
  24.6 0.7 copy-start.3
